TPU v7x, 256 devices: a whole 4x4x8 slice. The times are simulated.
256 devices in a mesh: ex: 64 (over x, z, core), lay: 4 (over y).
Axes of the slice: x: 4, y: 4, z: 8, core: 2. Of those that a mesh axis runs over, the one named last changes fastest.
Arguments:
- queries: bfloat16 [512, 4, 4096], P('ex', 'lay'), may hold values from -6 to 6
- train_mantissa: bfloat16 [81920, 4, 4096], P('ex', 'lay'), may hold values from -4 to 4
- scale_exponents: int32 [81920, 4, 32], P('ex', 'lay'), may hold values from -2 to 1
- basis_out: float32 [4, 64, 64], P('lay'), may hold values from -0.75 to 0.75
- basis_in: float32 [4, 64, 64], P('lay'), may hold values from -0.75 to 0.75
- eigen: float32 [4, 64, 64], P('lay'), may hold values from 0.5 to 4
- assignment: int32 [512], replicated, may hold values from 0 to 1, as said below
Outputs:
- scores: float32 [512, 81920], P('lay', 'ex')
- batch_totals: float32 [2, 81920], P(None, 'ex')
Inputs may be any that keep to these rules, and one draw needn't show every extreme that they name: `assignment`: each of the two batches holds exactly 256 queries.
All inputs are finite; a program needn't handle non-finite values.
Results may differ from a plain program's by a relative error of at most 0.003.
Values may be sent and summed in bfloat16 or wider, within the bound.
A program may use at most 128 MiB of HBM per device.

v0:
```python
import math

import jax
import jax.numpy as jnp
from jax import lax
from jax.experimental import pallas as pl
from jax.experimental.pallas import tpu as pltpu
from jax.sharding import PartitionSpec as P

MESH = pl.DeviceIdType.MESH
f32, bf16 = jnp.float32, jnp.bfloat16

NX, NY, NZ = 4, 4, 8
ORDER = 64
ENTRIES = ORDER * ORDER
HALF = ENTRIES // 2
BLOCKS = 32
BLOCK = ENTRIES // BLOCKS
ROWS = 1280
QDEV = 8
PAIR = 16
KA = 768
KB = HALF - KA
NT = 256
TCH = 128
NCH = ROWS // TCH
HT = ROWS // 2
QB = 256
lowest_exponent = -2
highest_exponent = 2

ZORDER = (0, 1, 7, 2, 6, 3, 5, 4)
ZSLOT = {zr: i for i, zr in enumerate(ZORDER)}
XORDER = (0, 1, 3, 2)
XSLOT = {xr: i for i, xr in enumerate(XORDER)}
XBLK = ((0, 1), (1, 2), (3, 1))
GROUPS = 4


def split(v):
    hi = v.astype(bf16)
    return hi, (v - hi.astype(f32)).astype(bf16)


def dot3(a, b, dims):
    (ah, al), (bh, bl) = a, b

    def one(u, v):
        return lax.dot_general(u, v, (dims, ((), ())), preferred_element_type=f32)

    out = one(ah, bh) + one(ah, bl)
    return out if al is None else out + one(al, bh)


def precondition(q_ref, bo_ref, bi_ref, eig_ref, bd, mid, out):
    bi = bi_ref[...]
    bd[...] = jnp.zeros((128, 128), f32)
    bd[0:64, 0:64] = bi
    bd[64:128, 64:128] = bi
    even, odd = bo_ref[pl.ds(0, 32, stride=2), :], bo_ref[pl.ds(1, 32, stride=2), :]
    q = q_ref[...]
    rows = jnp.concatenate(
        [q[:, b * BLOCK : (b + 1) * BLOCK].astype(f32) for b in range(BLOCKS)], axis=0
    ).astype(bf16)
    bds = split(bd[...])
    mid[...] = dot3((rows, None), bds, ((1,), (0,)))
    t1 = jnp.concatenate([mid[pl.ds(n, BLOCKS, stride=QDEV), :] for n in range(QDEV)], axis=1)
    y = dot3(split(jnp.concatenate([even, odd], axis=1).T), split(t1), ((1,), (0,)))
    low = lax.broadcasted_iota(jnp.int32, (64, 128), 1) < 64
    eig = jnp.concatenate([eig_ref[...], eig_ref[...]], axis=1)
    parts = []
    for n in range(QDEV):
        lanes = slice(n * 128, (n + 1) * 128)
        s = jnp.where(low, y[0:64, lanes], y[64:128, lanes])
        parts.append((s + pltpu.roll(s, 64, 1)) / eig)
    u = jnp.concatenate(parts, axis=1)
    v = dot3(split(jnp.concatenate([even, odd], axis=0)), split(u), ((1,), (0,)))
    low32 = lax.broadcasted_iota(jnp.int32, (32, 128), 1) < 64
    for n in range(QDEV):
        lanes = slice(n * 128, (n + 1) * 128)
        mid[pl.ds(n, BLOCKS, stride=QDEV), :] = jnp.where(low32, v[0:32, lanes], v[32:64, lanes])
    o = dot3(split(mid[...]), bds, ((1,), (1,)))
    for b in range(BLOCKS):
        out[:, b * BLOCK : (b + 1) * BLOCK] = o[QDEV * b : QDEV * (b + 1)]


def kernel(
    q_hbm, mant_hbm, exps_hbm, bo_hbm, bi_hbm, eig_hbm, asg_hbm,
    scores_hbm, totals_ref,
    q_ref, exps_ref, bo_ref, bi_ref, eig_ref, asg_ref,
    mant, w, pa, pb, acc, fac, mask, bd, mid, prep, xch,
    s2, r1a, r1b, s1p, s1m, r2p, r2m, tot, tot_in, out,
    ss, rs, ls, ms, os,
):
    e, y = lax.axis_index("ex"), lax.axis_index("lay")
    x, z, c = e // 16, (e // 2) % NZ, e % 2

    def at_x(d):
        return {"ex": (((x + d + NX) % NX) * NZ + z) * 2 + c}

    def at_z(d):
        return {"ex": (x * NZ + (z + d + NZ) % NZ) * 2 + c}

    def at_y(d):
        return {"lay": (y + d + NY) % NY}

    sibling = {"ex": (x * NZ + z) * 2 + 1 - c}

    small = [
        pltpu.make_async_copy(a, b, ls.at[i])
        for i, (a, b) in enumerate(
            (
                (q_hbm, q_ref), (bo_hbm, bo_ref), (bi_hbm, bi_ref),
                (eig_hbm, eig_ref), (exps_hbm, exps_ref), (asg_hbm, asg_ref),
            )
        )
    ]
    for cp in small:
        cp.start()
    loads = [
        pltpu.make_async_copy(
            mant_hbm.at[pl.ds(i * TCH, TCH)], mant.at[pl.ds(i * TCH, TCH)], ms.at[i]
        )
        for i in range(NCH)
    ]
    for cp in loads:
        cp.start()
    barrier = pltpu.get_barrier_semaphore()
    for dev in (at_x(1), at_x(-1), at_z(1), at_z(-1), at_y(1), at_y(-1), at_y(2), sibling):
        pl.semaphore_signal(barrier, inc=1, device_id=dev, device_id_type=MESH)

    copies, live = {}, []

    def remote(name, src, dst, dev):
        i = len(copies)
        copies[name] = pltpu.make_async_remote_copy(
            src_ref=src, dst_ref=dst, send_sem=ss.at[i], recv_sem=rs.at[i],
            device_id=dev, device_id_type=MESH,
        )

    def send(*name):
        copies[name].start()
        live.append(name)

    def arrived(*name):
        copies[name].wait_recv()

    def settle(keep=0):
        while len(live) > keep:
            copies[live.pop(0)].wait_send()

    for d in (1, -1):
        lo = 0 if d == 1 else 1
        bh = pl.ds(lo * (KB // 2), KB // 2)
        ah = pl.ds(lo * (KA // 2), KA // 2)
        for k in range(4):
            a, b = ZSLOT[(-d * k) % NZ], ZSLOT[(-d * (k + 1)) % NZ]
            lanes = bh if k == 3 else pl.ds(0, KB)
            remote(("bz", d, k), pb.at[0, a, 0, :, lanes], pb.at[0, b, 0, :, lanes], at_z(d))
            lanes = ah if k == 3 else pl.ds(0, KA)
            for i, (first, count) in enumerate(XBLK):
                blk = pl.ds(first, count)
                remote(
                    ("az", d, i, k), pa.at[0, a, blk, :, lanes], pa.at[0, b, blk, :, lanes], at_z(d)
                )
        near = XSLOT[(-d) % NX]
        for zr in range(NZ):
            s = ZSLOT[zr]
            remote(("bx", d, zr), pb.at[0, s, 0], pb.at[0, s, near], at_x(d))
            remote(("bx2", d, zr), pb.at[0, s, near, :, bh], pb.at[0, s, 3, :, bh], at_x(d))
        remote(("ax", d), pa.at[0, 0, 0], pa.at[0, 0, near], at_x(d))
        remote(("ax2", d), pa.at[0, 0, near, :, ah], pa.at[0, 0, 3, :, ah], at_x(d))
    for g in range(GROUPS):
        two = pl.ds(2 * g, 2)
        remote(("sa", g), pa.at[0, two], pa.at[1, two], sibling)
        remote(("sb", g), pb.at[0, two], pb.at[1, two], sibling)
        remote(("y2", 1, g), s2.at[g, :, :, pl.ds(0, HT)], r1a.at[g], at_y(1))
        remote(("y2", -1, g), s2.at[g, :, :, pl.ds(HT, HT)], r1b.at[g], at_y(-1))
        remote(("y1", 1, g), s1p.at[g], r2p.at[g], at_y(1))
        remote(("y1", -1, g), s1m.at[g], r2m.at[g], at_y(-1))
    for i, d in enumerate((1, -1, 2)):
        remote(("tot", d), tot, tot_in.at[i], at_y(d))
    other_cols = pl.ds(pl.multiple_of((1 - c) * HALF, HALF), HALF)
    own_cols = pl.ds(pl.multiple_of(c * HALF, HALF), HALF)
    remote(("swap",), prep.at[:, other_cols], xch.at[c], sibling)

    for cp in small:
        cp.wait()
    precondition(q_ref, bo_ref, bi_ref, eig_ref, bd, mid, prep)
    pl.semaphore_wait(barrier, 8)
    send("swap")
    exps = exps_ref[...]
    factor = jnp.zeros(exps.shape, f32)
    for exponent in range(lowest_exponent, highest_exponent):
        factor = factor + jnp.where(exps == exponent, f32(2.0**exponent), f32(0.0))
    fac[...] = factor
    for i in range(NX):
        one = (asg_ref[:, i * 128 : (i + 1) * 128] == 1).astype(f32)
        mask[i] = jnp.broadcast_to(one, (128, 128)).T

    def dequantize(first, count):
        for i in range(first, first + count):
            loads[i].wait()

        def step(i, carry):
            t = pl.ds(pl.multiple_of(i * TCH, TCH), TCH)
            for b in range(BLOCKS):
                rows = pl.ds(b * BLOCK, BLOCK)
                w[rows, t] = mant[t, rows].T * fac[b : b + 1, t].astype(bf16)
            return carry

        lax.fori_loop(first, first + count, step, 0)

    def multiply(g, h):
        part = c if h == 0 else 1 - c
        base = pl.multiple_of(part * HALF, HALF)
        two = pl.ds(2 * g, 2)

        def step(n, carry):
            cols = pl.ds(pl.multiple_of(n * NT, NT), NT)
            a = pa[h, two].reshape(128, KA)
            b = pb[h, two].reshape(128, KB)
            r = jnp.dot(a, w[pl.ds(base, KA), cols], preferred_element_type=f32)
            r = r + jnp.dot(
                b, w[pl.ds(pl.multiple_of(base + KA, 256), KB), cols], preferred_element_type=f32
            )
            r = r.reshape(2, NX, PAIR, NT)
            acc[g, :, :, :, cols] = r if h == 0 else acc[g, :, :, :, cols] + r
            return carry

        lax.fori_loop(0, ROWS // NT, step, 0)

    def slot_of(d):
        xr = (y + d + NY - x + NX) % NX
        return xr + xr // 2 - 2 * (xr // 3)

    def add_totals(g):
        t0, t1 = None, None
        for s in range(2):
            zo = (z + ZORDER[2 * g + s]) % NZ
            for j in range(NX):
                xo = (x + XORDER[j]) % NX
                m = mask[xo, pl.ds(pl.multiple_of(zo * PAIR, PAIR), PAIR), :]
                m = jnp.concatenate([m] * (ROWS // 128), axis=1)
                v = acc[g, s, j]
                p1 = v * m
                p0 = v - p1
                p0, p1 = p0[0:8] + p0[8:16], p1[0:8] + p1[8:16]
                t0, t1 = (p0, p1) if t0 is None else (t0 + p0, t1 + p1)
        both = jnp.concatenate(
            [
                jnp.sum(t0, axis=0, keepdims=True),
                jnp.sum(t1, axis=0, keepdims=True),
                jnp.zeros((6, ROWS), f32),
            ],
            axis=0,
        )
        tot[...] = both if g == 0 else tot[...] + both

    def reduce1(g):
        far = slot_of(2)
        for s in range(2):
            s2[g, s] = acc[g, s, far].astype(bf16)
        send("y2", 1, g)
        send("y2", -1, g)

    def reduce2(g):
        up, down = slot_of(1), slot_of(-1)
        arrived("y2", 1, g)
        for s in range(2):
            s1p[g, s, :, 0:HT] = (acc[g, s, up, :, 0:HT] + r1a[g, s].astype(f32)).astype(bf16)
            s1p[g, s, :, HT:ROWS] = acc[g, s, up, :, HT:ROWS].astype(bf16)
        send("y1", 1, g)
        arrived("y2", -1, g)
        for s in range(2):
            s1m[g, s, :, 0:HT] = acc[g, s, down, :, 0:HT].astype(bf16)
            s1m[g, s, :, HT:ROWS] = (
                acc[g, s, down, :, HT:ROWS] + r1b[g, s].astype(f32)
            ).astype(bf16)
        send("y1", -1, g)

    normalizer = 1.0 / math.sqrt(NY * ENTRIES)
    stores = []

    def reduce3(g):
        mine = slot_of(0)
        arrived("y1", 1, g)
        arrived("y1", -1, g)
        for s in range(2):
            total = acc[g, s, mine] + r2p[g, s].astype(f32) + r2m[g, s].astype(f32)
            out[g, s] = total * normalizer
            zo = (z + ZORDER[2 * g + s]) % NZ
            cp = pltpu.make_async_copy(
                out.at[g, s],
                scores_hbm.at[pl.ds(pl.multiple_of(zo * PAIR, PAIR), PAIR)],
                os.at[2 * g + s],
            )
            cp.start()
            stores.append(cp)

    def round_of(r):
        before = len(live)
        if r <= 4:
            for d in (1, -1):
                arrived("bz", d, r - 1)
                if r < 4:
                    send("bz", d, r)
            if r < 4:
                for d in (1, -1):
                    for e_ in (1, -1):
                        send("bx", e_, (-d * r) % NZ)
            else:
                for e_ in (1, -1):
                    send("bx", e_, 4)
        if r == 1:
            for d in (1, -1):
                arrived("ax", d)
                send("ax2", d)
            for d in (1, -1):
                send("az", d, 1, 0)
        if r == 2:
            for d in (1, -1):
                arrived("ax2", d)
            for d in (1, -1):
                send("az", d, 2, 0)
        for i in range(3):
            k = r - 1 - i
            if 0 <= k <= 3:
                for d in (1, -1):
                    arrived("az", d, i, k)
                    if k < 3:
                        send("az", d, i, k + 1)
        if r <= 5:
            for zr in sorted({(r - 1) % NZ, (1 - r) % NZ}):
                for d in (1, -1):
                    arrived("bx", d, zr)
                    send("bx2", d, zr)
        if 2 <= r:
            for zr in sorted({(r - 2) % NZ, (2 - r) % NZ}):
                for d in (1, -1):
                    arrived("bx2", d, zr)
        settle(len(live) - before)

    def share(g):
        send("sa", g)
        send("sb", g)

    def shared(g):
        arrived("sa", g)
        arrived("sb", g)

    xch[c] = prep[:, own_cols]
    arrived("swap")
    both = xch[...].reshape(PAIR, HALF).astype(bf16)
    pa[0, 0, 0] = both[:, 0:KA]
    pb[0, 0, 0] = both[:, KA:HALF]
    for d in (1, -1):
        send("bz", d, 0)
    for d in (1, -1):
        send("ax", d)
    for d in (1, -1):
        send("bx", d, 0)
    for d in (1, -1):
        send("az", d, 0, 0)

    dequantize(0, 4)
    round_of(1)
    dequantize(4, 3)
    round_of(2)
    dequantize(7, 3)
    round_of(3)
    share(0)
    multiply(0, 0)
    round_of(4)
    share(1)
    shared(0)
    multiply(0, 1)
    reduce1(0)
    add_totals(0)
    multiply(1, 0)
    round_of(5)
    share(2)
    shared(1)
    multiply(1, 1)
    reduce2(0)
    reduce1(1)
    add_totals(1)
    multiply(2, 0)
    round_of(6)
    share(3)
    reduce3(0)
    shared(2)
    multiply(2, 1)
    reduce2(1)
    reduce1(2)
    add_totals(2)
    multiply(3, 0)
    shared(3)
    multiply(3, 1)
    reduce1(3)
    add_totals(3)
    for d in (1, -1, 2):
        send("tot", d)
    reduce2(2)
    reduce3(1)
    reduce2(3)
    reduce3(2)
    for d in (1, -1, 2):
        arrived("tot", d)
    total = tot[...] + tot_in[0] + tot_in[1] + tot_in[2]
    totals_ref[...] = total[0:2] * (normalizer / math.sqrt(QB))
    reduce3(3)
    settle()
    for cp in stores:
        cp.wait()


N_COPIES = 2 * (4 + 12 + 16 + 2) + GROUPS * 6 + 3 + 1


def body(queries, train_mantissa, scale_exponents, basis_out, basis_in, eigen, assignment):
    hbm = pl.BlockSpec(memory_space=pl.ANY)
    vmem = pltpu.VMEM
    dma = pltpu.SemaphoreType.DMA
    piece = (GROUPS, 2, PAIR, ROWS)
    scores, totals = pl.pallas_call(
        kernel,
        out_shape=(
            jax.ShapeDtypeStruct((NX * 32, ROWS), f32),
            jax.ShapeDtypeStruct((2, ROWS), f32),
        ),
        in_specs=[hbm] * 7,
        out_specs=(hbm, pl.BlockSpec(memory_space=pltpu.VMEM)),
        scratch_shapes=[
            vmem((QDEV, ENTRIES), bf16),
            vmem((BLOCKS, ROWS), jnp.int32),
            vmem((ORDER, ORDER), f32),
            vmem((ORDER, ORDER), f32),
            vmem((ORDER, ORDER), f32),
            vmem((1, 512), jnp.int32),
            vmem((ROWS, ENTRIES), bf16),
            vmem((ENTRIES, ROWS), bf16),
            vmem((2, NZ, NX, PAIR, KA), bf16),
            vmem((2, NZ, NX, PAIR, KB), bf16),
            vmem((GROUPS, 2, NX, PAIR, ROWS), f32),
            vmem((BLOCKS, ROWS), f32),
            vmem((NX, 128, 128), f32),
            vmem((128, 128), f32),
            vmem((BLOCKS * QDEV, 128), f32),
            vmem((QDEV, ENTRIES), f32),
            vmem((2, QDEV, HALF), f32),
            vmem(piece, bf16),
            vmem((GROUPS, 2, PAIR, HT), bf16),
            vmem((GROUPS, 2, PAIR, HT), bf16),
            vmem(piece, bf16),
            vmem(piece, bf16),
            vmem(piece, bf16),
            vmem(piece, bf16),
            vmem((8, ROWS), f32),
            vmem((3, 8, ROWS), f32),
            vmem(piece, f32),
            dma((N_COPIES,)),
            dma((N_COPIES,)),
            dma((6,)),
            dma((NCH,)),
            dma((2 * GROUPS,)),
        ],
        compiler_params=pltpu.CompilerParams(
            collective_id=0, has_side_effects=True, vmem_limit_bytes=56 * 2**20
        ),
        name="influence",
    )(
        queries.reshape(QDEV, ENTRIES),
        train_mantissa.reshape(ROWS, ENTRIES),
        scale_exponents.reshape(ROWS, BLOCKS).T,
        basis_out.reshape(ORDER, ORDER),
        basis_in.reshape(ORDER, ORDER),
        eigen.reshape(ORDER, ORDER),
        assignment.reshape(1, 512),
    )
    return scores, totals


def solution(mesh):
    placed = (
        P("ex", "lay", None),
        P("ex", "lay", None),
        P("ex", "lay", None),
        P("lay", None, None),
        P("lay", None, None),
        P("lay", None, None),
        P(),
    )
    return jax.shard_map(
        body, mesh=mesh, in_specs=placed, out_specs=(P("lay", "ex"), P(None, "ex")), check_vma=False
    )
```

profile of v0, /device:TPU:8, one launch (start us, length us, event | category | flops | bytes accessed | tf_op | source)
XLA Modules:
  0.0 58.1 jit_solution(16928800243739124415)
XLA Ops:
  0.6 54.2 %influence.1 = (f32[128,1280]{1,0:T(8,128)}, f32[2,1280]{1,0:T(2,128)}) custom-call(bf16[8,4096]{1,0:T(8,128)(2,1)} %bitcast.11, bf16[1280,4096]{1,0:T(8,128)(2,1)} %bitcast.9, s32[32,1280]{1,0:T(8,128)} %bitcast.10, f32[64,64]{1,0:T(8,128)} %bitcast.12, f32[64,64]{1,0:T(8,128)} %bitcast.13, f32[64,64]{1,0:T(8,128)} %bitcast.14, s32[1,512]{1,0:T(1,128)} %bitcast.15), custom_call_target="tpu_custom_call" | custom-call | tf_op jit(solution)/shard_map/influence/pallas_call | solution.py:426
  54.8 2.0 %copy.11 = f32[128,1280]{1,0:T(8,128)} copy(f32[128,1280]{1,0:T(8,128)} %get-tuple-element.4) | data formatting | bytes 1310720
  56.8 1.3 %copy.12 = f32[2,1280]{1,0:T(2,128)} copy(f32[2,1280]{1,0:T(2,128)} %get-tuple-element.5) | data formatting | bytes 20480
where the time goes:
time: 58.3 us; the launch traced here: 58.1 us
  Pallas kernels  54.2 us (93%)
  local copies, waits for them, and re-layouts  3.27 us (6%)
  between operations  0.64 us (1%)
    pallas_call x1, Pallas kernels, body(): pl.pallas_call(kernel, out_shape=(jax.ShapeDtypeStruct((NX * 32, ROWS), f...  54.2 us
    unnamed x2, local copies, waits for them, and re-layouts  3.27 us

commit v1 on v0

v1 whole, which is shorter than its diff:
```python
import math

import jax
import jax.numpy as jnp
from jax import lax
from jax.experimental import pallas as pl
from jax.experimental.pallas import tpu as pltpu
from jax.sharding import PartitionSpec as P

MESH = pl.DeviceIdType.MESH
f32, bf16 = jnp.float32, jnp.bfloat16

NX, NY, NZ = 4, 4, 8
ORDER = 64
ENTRIES = ORDER * ORDER
HALF = ENTRIES // 2
BLOCKS = 32
BLOCK = ENTRIES // BLOCKS
ROWS = 1280
QDEV = 8
PAIR = 16
KA = 1024
KB = HALF - KA
NT = 256
TCH = 128
NCH = ROWS // TCH
EARLY = 2
QB = 256
lowest_exponent = -2
highest_exponent = 2

ZORDER = (0, 1, 7, 2, 6, 3, 5, 4)
ZSLOT = {zr: i for i, zr in enumerate(ZORDER)}
XORDER = (0, 1, 3, 2)
XSLOT = {xr: i for i, xr in enumerate(XORDER)}
XBLK = ((0, 1), (1, 2), (3, 1))
DIST = ((0, 1), (1, 2), (3, 2), (5, 2), (7, 1))
GROUP = ((0, 1), (1, 2), (3, 2), (5, 2), (7, 1))
Z_STEP = ()
A_STEP = (2, 3)
X_FAR = (0, 1)
STEPS = (
    (('copy',), (), (('bz', 1, 1), ('bz', -1, 1), ('bx', 1, 0), ('bx', -1, 0), ('bx2', 2, 0), ('ax', 1), ('ax', -1), ('ax', 2), ('bz', 1, 2), ('bz', -1, 2), ('az', 1, 0, 1), ('az', -1, 0, 1), ('bz', 1, 3), ('bz', -1, 3))),
    (('dq', 0), (), ()),
    (('dq', 1), (), ()),
    (('dq', 2), (), ()),
    (('dq', 3), (), ()),
    (('dq', 4), (), ()),
    (('dq', 5), (), ()),
    (('dq', 6), (), ()),
    (('dq', 7), (), ()),
    (('dq', 8), (), ()),
    (('copy',), (('bz', 1, 1), ('bz', -1, 1)), (('bx', 1, 1), ('bx', -1, 1), ('bx2', 2, 1))),
    (('dq', 9), (), ()),
    (('copy',), (('ax', 1), ('ax', -1)), (('az', 1, 1, 1), ('az', -1, 1, 1))),
    (('copy',), (('az', 1, 0, 1),), (('az', 1, 0, 2),)),
    (('copy',), (('az', -1, 0, 1),), (('az', -1, 0, 2),)),
    (('copy',), (('ax', 2), ('bx', 1, 0), ('bx', -1, 0), ('bx2', 2, 0)), (('sh', 0),)),
    (('copy',), (), (('az', 1, 2, 1), ('az', -1, 2, 1))),
    (('mma', 0, 0), (), ()),
    (('mma', 0, 1), (), ()),
    (('mma', 0, 2), (), ()),
    (('copy',), (('bz', 1, 2), ('bz', -1, 2)), (('bx', 1, 2), ('bx', -1, 2))),
    (('mma', 0, 3), (), ()),
    (('mma', 0, 4), (), ()),
    (('settle', 8), (), ()),
    (('mmb', 0, 0), (('sh', 0),), ()),
    (('mmb', 0, 1), (), ()),
    (('copy',), (('bz', 1, 3),), (('bz4', 1),)),
    (('copy',), (('bz', -1, 3),), (('bx', 1, 3), ('bx', -1, 3))),
    (('copy',), (), (('bz4', -1),)),
    (('mmb', 0, 2), (), ()),
    (('mmb', 0, 3), (), ()),
    (('mmb', 0, 4), (), ()),
    (('scatter', 0), (), (('part', 2, 0), ('part', 1, 0), ('part', -1, 0))),
    (('tot', 0), (), ()),
    (('settle', 6), (), ()),
    (('copy',), (('az', 1, 1, 1),), (('az', 1, 1, 2),)),
    (('copy',), (('az', -1, 1, 1),), (('az', -1, 1, 2),)),
    (('copy',), (('az', 1, 0, 2),), (('az', 1, 0, 3),)),
    (('copy',), (('az', -1, 0, 2),), (('az', -1, 0, 3),)),
    (('settle', 3), (), ()),
    (('copy',), (('az', 1, 2, 1),), (('az', 1, 2, 2),)),
    (('copy',), (('az', -1, 2, 1),), (('az', -1, 2, 2),)),
    (('copy',), (('bx', -1, 2),), (('bx2', -1, 2),)),
    (('copy',), (('bx', 1, 2),), (('bx2', 1, 2),)),
    (('copy',), (('bx', 1, 1), ('bx', -1, 1), ('bx2', 2, 1)), (('sh', 1),)),
    (('mma', 1, 0), (), ()),
    (('mma', 1, 1), (), ()),
    (('copy',), (('bz4', 1), ('bz4', -1)), (('bx', 1, 4), ('bx', -1, 4))),
    (('mma', 1, 2), (), ()),
    (('mma', 1, 3), (), ()),
    (('mma', 1, 4), (), ()),
    (('copy',), (('bx', 1, 3),), (('bx2', 1, 3),)),
    (('copy',), (('bx', -1, 3),), (('bx2', -1, 3),)),
    (('settle', 9), (), ()),
    (('collect', 0), (('part', 1, 0), ('part', -1, 0), ('part', 2, 0)), ()),
    (('copy',), (('az', 1, 1, 2),), (('az', 1, 1, 3),)),
    (('copy',), (('az', -1, 1, 2),), (('az', -1, 1, 3),)),
    (('mmb', 1, 0), (('sh', 1),), ()),
    (('mmb', 1, 1), (), ()),
    (('mmb', 1, 2), (), ()),
    (('mmb', 1, 3), (), ()),
    (('mmb', 1, 4), (), ()),
    (('scatter', 1), (), (('part', 2, 1), ('part', 1, 1), ('part', -1, 1))),
    (('copy',), (('az', 1, 0, 3),), (('az4', 1, 0),)),
    (('copy',), (('az', -1, 0, 3),), (('az4', -1, 0),)),
    (('copy',), (('az', 1, 2, 2),), (('az', 1, 2, 3),)),
    (('copy',), (('bx2', 1, 2), ('bx2', -1, 2), ('az', -1, 2, 2)), (('sh', 2),)),
    (('copy',), (), (('az', -1, 2, 3),)),
    (('copy',), (('bx', -1, 4),), (('bx2', -1, 4),)),
    (('copy',), (('bx', 1, 4),), (('bx2', 1, 4),)),
    (('tot', 1), (), ()),
    (('mma', 2, 0), (), ()),
    (('mma', 2, 1), (), ()),
    (('mma', 2, 2), (), ()),
    (('mma', 2, 3), (), ()),
    (('mma', 2, 4), (), ()),
    (('settle', 11), (), ()),
    (('mmb', 2, 0), (('sh', 2),), ()),
    (('copy',), (('az', 1, 1, 3),), (('az4', 1, 1),)),
    (('mmb', 2, 1), (), ()),
    (('mmb', 2, 2), (), ()),
    (('mmb', 2, 3), (), ()),
    (('mmb', 2, 4), (), ()),
    (('scatter', 2), (), (('part', 2, 2), ('part', 1, 2), ('part', -1, 2))),
    (('copy',), (('az', 1, 2, 3),), (('az4', 1, 2),)),
    (('copy',), (('bx2', 1, 3), ('bx2', -1, 3), ('az', -1, 1, 3), ('az', -1, 2, 3)), (('sh', 3),)),
    (('copy',), (), (('az4', -1, 2),)),
    (('mma', 3, 0), (), ()),
    (('mma', 3, 1), (), ()),
    (('mma', 3, 2), (), ()),
    (('mma', 3, 3), (), ()),
    (('copy',), (), (('az4', -1, 1),)),
    (('tot', 2), (), ()),
    (('mma', 3, 4), (), ()),
    (('settle', 11), (), ()),
    (('collect', 1), (('part', 1, 1), ('part', -1, 1), ('part', 2, 1)), ()),
    (('mmb', 3, 0), (('sh', 3),), ()),
    (('mmb', 3, 1), (), ()),
    (('mmb', 3, 2), (), ()),
    (('mmb', 3, 3), (), ()),
    (('mmb', 3, 4), (), ()),
    (('scatter', 3), (), (('part', 2, 3), ('part', 1, 3), ('part', -1, 3))),
    (('tot', 3), (), ()),
    (('settle', 6), (), ()),
    (('copy',), (('bx2', 1, 4), ('bx2', -1, 4), ('az4', 1, 0), ('az4', 1, 1), ('az4', 1, 2), ('az4', -1, 0), ('az4', -1, 1), ('az4', -1, 2)), (('sh', 4),)),
    (('mma', 4, 0), (), ()),
    (('mma', 4, 1), (), ()),
    (('mma', 4, 2), (), ()),
    (('mma', 4, 3), (), ()),
    (('mma', 4, 4), (), ()),
    (('settle', 5), (), ()),
    (('mmb', 4, 0), (('sh', 4),), ()),
    (('collect', 2), (('part', 1, 2), ('part', -1, 2), ('part', 2, 2)), ()),
    (('mmb', 4, 1), (), ()),
    (('mmb', 4, 2), (), ()),
    (('mmb', 4, 3), (), ()),
    (('mmb', 4, 4), (), ()),
    (('scatter', 4), (), (('part', 2, 4), ('part', 1, 4), ('part', -1, 4))),
    (('tot', 4), (), (('tot', 1), ('tot', -1), ('tot', 2))),
    (('settle', 7), (), ()),
    (('collect', 3), (('part', 1, 3), ('part', -1, 3), ('part', 2, 3)), ()),
    (('settle', 4), (), ()),
    (('collect', 4), (('part', 1, 4), ('part', -1, 4), ('part', 2, 4)), ()),
)


def split(v):
    hi = v.astype(bf16)
    return hi, (v - hi.astype(f32)).astype(bf16)


def dot3(a, b, dims):
    (ah, al), (bh, bl) = a, b

    def one(u, v):
        return lax.dot_general(u, v, (dims, ((), ())), preferred_element_type=f32)

    out = one(ah, bh) + one(ah, bl)
    return out if al is None else out + one(al, bh)


def precondition(q_ref, bo_ref, bi_ref, eig_ref, bd, mid, out):
    bi = bi_ref[...]
    bd[...] = jnp.zeros((128, 128), f32)
    bd[0:64, 0:64] = bi
    bd[64:128, 64:128] = bi
    even, odd = bo_ref[pl.ds(0, 32, stride=2), :], bo_ref[pl.ds(1, 32, stride=2), :]
    q = q_ref[...]
    rows = jnp.concatenate(
        [q[:, b * BLOCK : (b + 1) * BLOCK].astype(f32) for b in range(BLOCKS)], axis=0
    ).astype(bf16)
    bds = split(bd[...])
    mid[...] = dot3((rows, None), bds, ((1,), (0,)))
    t1 = jnp.concatenate([mid[pl.ds(n, BLOCKS, stride=QDEV), :] for n in range(QDEV)], axis=1)
    y = dot3(split(jnp.concatenate([even, odd], axis=1).T), split(t1), ((1,), (0,)))
    low = lax.broadcasted_iota(jnp.int32, (64, 128), 1) < 64
    eig = jnp.concatenate([eig_ref[...], eig_ref[...]], axis=1)
    parts = []
    for n in range(QDEV):
        lanes = slice(n * 128, (n + 1) * 128)
        s = jnp.where(low, y[0:64, lanes], y[64:128, lanes])
        parts.append((s + pltpu.roll(s, 64, 1)) / eig)
    u = jnp.concatenate(parts, axis=1)
    v = dot3(split(jnp.concatenate([even, odd], axis=0)), split(u), ((1,), (0,)))
    low32 = lax.broadcasted_iota(jnp.int32, (32, 128), 1) < 64
    for n in range(QDEV):
        lanes = slice(n * 128, (n + 1) * 128)
        mid[pl.ds(n, BLOCKS, stride=QDEV), :] = jnp.where(low32, v[0:32, lanes], v[32:64, lanes])
    o = dot3(split(mid[...]), bds, ((1,), (1,)))
    for b in range(BLOCKS):
        out[:, b * BLOCK : (b + 1) * BLOCK] = o[QDEV * b : QDEV * (b + 1)]


def kernel(
    q_hbm, mant_hbm, exps_hbm, bo_hbm, bi_hbm, eig_hbm, asg_hbm,
    scores_hbm, totals_ref,
    q_ref, exps_ref, bo_ref, bi_ref, eig_ref, asg_ref,
    mant, w, p, acc, fac, mask, bd, mid, prep, xch,
    part_out, part_in, sums, tot, tot_in, out,
    ss, rs, ls, ms, os,
):
    e, y = lax.axis_index("ex"), lax.axis_index("lay")
    x, z, c = e // 16, (e // 2) % NZ, e % 2

    def at_x(d):
        return {"ex": (((x + d + NX) % NX) * NZ + z) * 2 + c}

    def at_z(d):
        return {"ex": (x * NZ + (z + d + NZ) % NZ) * 2 + c}

    def at_y(d):
        return {"lay": (y + d + NY) % NY}

    sibling = {"ex": (x * NZ + z) * 2 + 1 - c}

    small = [
        pltpu.make_async_copy(a, b, ls.at[i])
        for i, (a, b) in enumerate(
            (
                (q_hbm, q_ref), (bo_hbm, bo_ref), (bi_hbm, bi_ref),
                (eig_hbm, eig_ref), (exps_hbm, exps_ref), (asg_hbm, asg_ref),
            )
        )
    ]
    for cp in small:
        cp.start()
    loads = [
        pltpu.make_async_copy(
            mant_hbm.at[pl.ds(i * TCH, TCH)], mant.at[pl.ds(i * TCH, TCH)], ms.at[i]
        )
        for i in range(NCH)
    ]
    for cp in loads:
        cp.start()
    barrier = pltpu.get_barrier_semaphore()
    partners = [at_x(d) for d in (1, -1, 2)] + [at_y(d) for d in (1, -1, 2)]
    partners += [at_z(d * k) for k in (1, 2, 3) for d in (1, -1)] + [sibling]
    for dev in partners:
        pl.semaphore_signal(barrier, inc=1, device_id=dev, device_id_type=MESH)

    copies, live = {}, []

    def remote(name, src, dst, dev):
        i = len(copies)
        copies[name] = pltpu.make_async_remote_copy(
            src_ref=src, dst_ref=dst, send_sem=ss.at[i], recv_sem=rs.at[i],
            device_id=dev, device_id_type=MESH,
        )

    def send(*name):
        copies[name].start()
        live.append(name)

    def arrived(*name):
        copies[name].wait_recv()

    def settle(keep=0):
        while len(live) > keep:
            copies[live.pop(0)].wait_send()

    def lanes(first, count):
        return pl.ds(pl.multiple_of(c * HALF + first, 128), count)

    la, lb, lhalf = lanes(0, KA), lanes(KA, KB), lanes(0, HALF)
    for d in (1, -1):
        hi = 0 if d == 1 else 1
        la2 = lanes(hi * (KA // 2), KA // 2)
        lb2 = lanes(KA + hi * (KB // 2), KB // 2)
        hops = [ZSLOT[(-d * k) % NZ] for k in (0, 1, 2, 3)]
        for k in (1, 2, 3):
            via = k - 1 if k in Z_STEP else 0
            remote(
                ("bz", d, k), p.at[hops[via], 0, :, lb], p.at[hops[k], 0, :, lb], at_z(d * (k - via))
            )
        remote(("bz4", d), p.at[hops[3], 0, :, lb2], p.at[ZSLOT[4], 0, :, lb2], at_z(d))
        for i, (first, count) in enumerate(XBLK):
            blk = pl.ds(first, count)
            for k in (1, 2, 3):
                via = k - 1 if k in A_STEP else 0
                remote(
                    ("az", d, i, k),
                    p.at[hops[via], blk, :, la], p.at[hops[k], blk, :, la], at_z(d * (k - via)),
                )
            remote(("az4", d, i), p.at[hops[3], blk, :, la2], p.at[ZSLOT[4], blk, :, la2], at_z(d))
        near = XSLOT[(-d) % NX]
        for i, (first, count) in enumerate(DIST):
            blk = pl.ds(first, count)
            remote(("bx", d, i), p.at[blk, 0, :, lb], p.at[blk, near, :, lb], at_x(d))
            if i not in X_FAR:
                remote(("bx2", d, i), p.at[blk, near, :, lb2], p.at[blk, 3, :, lb2], at_x(d))
            elif d == 1:
                remote(("bx2", 2, i), p.at[blk, 0, :, lb], p.at[blk, 3, :, lb], at_x(2))
        remote(("ax", d), p.at[0, 0, :, la], p.at[0, near, :, la], at_x(d))
    remote(("ax", 2), p.at[0, 0, :, la], p.at[0, 3, :, la], at_x(2))
    for g, (first, count) in enumerate(GROUP):
        blk = pl.ds(first, count)
        remote(("sh", g), p.at[blk, :, :, lhalf], p.at[blk, :, :, lhalf], sibling)
        for i, d in enumerate((1, -1, 2)):
            remote(("part", d, g), part_out.at[i, blk], part_in.at[i, blk], at_y(d))
    for i, d in enumerate((1, -1, 2)):
        remote(("tot", d), tot, tot_in.at[i], at_y(d))
    other_cols = pl.ds(pl.multiple_of((1 - c) * HALF, HALF), HALF)
    own_cols = pl.ds(pl.multiple_of(c * HALF, HALF), HALF)
    remote(("swap",), prep.at[:, other_cols], xch.at[c], sibling)

    for cp in small:
        cp.wait()
    precondition(q_ref, bo_ref, bi_ref, eig_ref, bd, mid, prep)
    pl.semaphore_wait(barrier, len(partners))
    send("swap")
    exps = exps_ref[...]
    factor = jnp.zeros(exps.shape, f32)
    for exponent in range(lowest_exponent, highest_exponent):
        factor = factor + jnp.where(exps == exponent, f32(2.0**exponent), f32(0.0))
    fac[...] = factor
    for i in range(NX):
        one = (asg_ref[:, i * 128 : (i + 1) * 128] == 1).astype(f32)
        mask[i] = jnp.broadcast_to(one, (128, 128)).T

    def dequantize(i):
        loads[i].wait()
        t = pl.ds(i * TCH, TCH)
        for b in range(BLOCKS):
            rows = pl.ds(b * BLOCK, BLOCK)
            w[rows, t] = mant[t, rows].T * fac[b : b + 1, t].astype(bf16)

    def multiply(g, n, part):
        first, count = GROUP[g]
        blk = pl.ds(first, count)
        k = pl.ds(pl.multiple_of((c if part == 0 else 1 - c) * HALF, HALF), HALF)
        cols = pl.ds(n * NT, NT)
        rows = count * NX * PAIR
        a = p[blk, :, :, k].reshape(rows, HALF)
        if rows < 128:
            a = jnp.concatenate([a, jnp.zeros((128 - rows, HALF), bf16)], axis=0)
        r = jnp.dot(a, w[k, cols], preferred_element_type=f32)[0:rows]
        r = r.reshape(count, NX, PAIR, NT)
        acc[blk, :, :, cols] = r if part == 0 else acc[blk, :, :, cols] + r

    def slot_of(d):
        xr = (y + d + NY - x + NX) % NX
        return xr + xr // 2 - 2 * (xr // 3)

    def add_totals(g):
        t0, t1 = None, None
        first, count = GROUP[g]
        for s in range(first, first + count):
            zo = (z + ZORDER[s]) % NZ
            for j in range(NX):
                xo = (x + XORDER[j]) % NX
                m = mask[xo, pl.ds(pl.multiple_of(zo * PAIR, PAIR), PAIR), :]
                m = jnp.concatenate([m] * (ROWS // 128), axis=1)
                v = acc[s, j]
                p1 = v * m
                p0 = v - p1
                p0, p1 = p0[0:8] + p0[8:16], p1[0:8] + p1[8:16]
                t0, t1 = (p0, p1) if t0 is None else (t0 + p0, t1 + p1)
        for i, t in enumerate((t0, t1)):
            sums[i] = t if g == 0 else sums[i] + t
        if g == len(GROUP) - 1:
            tot[...] = jnp.zeros(tot.shape, f32)
            for i in range(2):
                total = jnp.sum(sums[i], axis=0, keepdims=True)
                for n in range(ROWS // NT):
                    tot[8 * i + n : 8 * i + n + 1, :] = total[:, n * NT : (n + 1) * NT]

    def scatter(g):
        first, count = GROUP[g]
        for i, d in ((2, 2), (0, 1), (1, -1)):
            to = slot_of(d)
            for s in range(first, first + count):
                part_out[i, s] = acc[s, to].astype(bf16)

    normalizer = 1.0 / math.sqrt(NY * ENTRIES)
    stores = []

    def collect(g):
        mine = slot_of(0)
        first, count = GROUP[g]
        for s in range(first, first + count):
            total = acc[s, mine] + part_in[0, s].astype(f32)
            total = total + part_in[1, s].astype(f32) + part_in[2, s].astype(f32)
            out[s] = total * normalizer
            zo = (z + ZORDER[s]) % NZ
            cp = pltpu.make_async_copy(
                out.at[s],
                scores_hbm.at[pl.ds(pl.multiple_of(zo * PAIR, PAIR), PAIR)],
                os.at[s],
            )
            cp.start()
            stores.append(cp)

    do = {
        "copy": lambda: None, "settle": lambda n: settle(max(len(live) - n, 0)),
        "dq": lambda i: None if i < EARLY else dequantize(i),
        "mma": lambda g, n: multiply(g, n, 0), "mmb": lambda g, n: multiply(g, n, 1),
        "scatter": scatter, "tot": add_totals, "collect": collect,
    }
    xch[c] = prep[:, own_cols]
    for i in range(EARLY):
        dequantize(i)
    arrived("swap")
    p[0, 0, :, lhalf] = xch[...].reshape(PAIR, HALF).astype(bf16)
    for (step, *args), waits, sends in STEPS:
        for name in waits:
            arrived(*name)
        do[step](*args)
        for name in sends:
            send(*name)
    for d in (1, -1, 2):
        arrived("tot", d)
    total = tot[...] + tot_in[0] + tot_in[1] + tot_in[2]
    for i in range(2):
        for n in range(ROWS // NT):
            row = total[8 * i + n : 8 * i + n + 1, :]
            totals_ref[i : i + 1, n * NT : (n + 1) * NT] = row * (normalizer / math.sqrt(QB))
    settle()
    for cp in stores:
        cp.wait()


N_COPIES = 2 * (3 + 1 + 4 * len(XBLK) + 10 + 1) - len(X_FAR) + 1 + 4 * len(GROUP) + 3 + 1


def body(queries, train_mantissa, scale_exponents, basis_out, basis_in, eigen, assignment):
    hbm = pl.BlockSpec(memory_space=pl.ANY)
    vmem = pltpu.VMEM
    dma = pltpu.SemaphoreType.DMA
    piece = (3, NZ, PAIR, ROWS)
    scores, totals = pl.pallas_call(
        kernel,
        out_shape=(
            jax.ShapeDtypeStruct((NX * 32, ROWS), f32),
            jax.ShapeDtypeStruct((2, ROWS), f32),
        ),
        in_specs=[hbm] * 7,
        out_specs=(hbm, pl.BlockSpec(memory_space=pltpu.VMEM)),
        scratch_shapes=[
            vmem((QDEV, ENTRIES), bf16),
            vmem((BLOCKS, ROWS), jnp.int32),
            vmem((ORDER, ORDER), f32),
            vmem((ORDER, ORDER), f32),
            vmem((ORDER, ORDER), f32),
            vmem((1, 512), jnp.int32),
            vmem((ROWS, ENTRIES), bf16),
            vmem((ENTRIES, ROWS), bf16),
            vmem((NZ, NX, PAIR, ENTRIES), bf16),
            vmem((NZ, NX, PAIR, ROWS), f32),
            vmem((BLOCKS, ROWS), f32),
            vmem((NX, 128, 128), f32),
            vmem((128, 128), f32),
            vmem((BLOCKS * QDEV, 128), f32),
            vmem((QDEV, ENTRIES), f32),
            vmem((2, QDEV, HALF), f32),
            vmem(piece, bf16),
            vmem(piece, bf16),
            vmem((2, 8, ROWS), f32),
            vmem((16, NT), f32),
            vmem((3, 16, NT), f32),
            vmem((NZ, PAIR, ROWS), f32),
            dma((N_COPIES,)),
            dma((N_COPIES,)),
            dma((6,)),
            dma((NCH,)),
            dma((NZ,)),
        ],
        compiler_params=pltpu.CompilerParams(
            collective_id=0, has_side_effects=True, vmem_limit_bytes=56 * 2**20
        ),
        name="influence",
    )(
        queries.reshape(QDEV, ENTRIES),
        train_mantissa.reshape(ROWS, ENTRIES),
        scale_exponents.reshape(ROWS, BLOCKS).T,
        basis_out.reshape(ORDER, ORDER),
        basis_in.reshape(ORDER, ORDER),
        eigen.reshape(ORDER, ORDER),
        assignment.reshape(1, 512),
    )
    return scores, totals


def solution(mesh):
    placed = (
        P("ex", "lay", None),
        P("ex", "lay", None),
        P("ex", "lay", None),
        P("lay", None, None),
        P("lay", None, None),
        P("lay", None, None),
        P(),
    )
    return jax.shard_map(
        body, mesh=mesh, in_specs=placed, out_specs=(P("lay", "ex"), P(None, "ex")), check_vma=False
    )
```

time: 58.3 us -> 49.3 us (0.85)
  the two profiles are of different devices: /device:TPU:8 before, /device:TPU:1 now
where the time goes in v1:
time: 49.3 us; the launch traced here: 49.1 us
  Pallas kernels  45.2 us (92%)
  local copies, waits for them, and re-layouts  3.27 us (7%)
  between operations  0.64 us (1%)
    pallas_call x1, Pallas kernels, body(): pl.pallas_call(kernel, out_shape=(jax.ShapeDtypeStruct((NX * 32, ROWS), f...  45.2 us
    unnamed x2, local copies, waits for them, and re-layouts  3.27 us

profile of v1, /device:TPU:1, one launch (start us, length us, event | category | flops | bytes accessed | tf_op | source)
XLA Modules:
  0.0 49.1 jit_solution(18092297686628159560)
XLA Ops:
  0.6 45.2 %influence.1 = (f32[128,1280]{1,0:T(8,128)}, f32[2,1280]{1,0:T(2,128)}) custom-call(bf16[8,4096]{1,0:T(8,128)(2,1)} %bitcast.11, bf16[1280,4096]{1,0:T(8,128)(2,1)} %bitcast.9, s32[32,1280]{1,0:T(8,128)} %bitcast.10, f32[64,64]{1,0:T(8,128)} %bitcast.12, f32[64,64]{1,0:T(8,128)} %bitcast.13, f32[64,64]{1,0:T(8,128)} %bitcast.14, s32[1,512]{1,0:T(1,128)} %bitcast.15), custom_call_target="tpu_custom_call" | custom-call | tf_op jit(solution)/shard_map/influence/pallas_call | solution.py:452
  45.8 2.0 %copy.11 = f32[128,1280]{1,0:T(8,128)} copy(f32[128,1280]{1,0:T(8,128)} %get-tuple-element.4) | data formatting | bytes 1310720
  47.8 1.3 %copy.12 = f32[2,1280]{1,0:T(2,128)} copy(f32[2,1280]{1,0:T(2,128)} %get-tuple-element.5) | data formatting | bytes 20480

commit v2 on v1

--- a/solution.py
+++ b/solution.py
@@ -22,6 +22,7 @@
 KA = 1024
 KB = HALF - KA
 NT = 256
+HT = ROWS // 2
 TCH = 128
 NCH = ROWS // TCH
 EARLY = 2
@@ -36,11 +37,13 @@
 XBLK = ((0, 1), (1, 2), (3, 1))
 DIST = ((0, 1), (1, 2), (3, 2), (5, 2), (7, 1))
 GROUP = ((0, 1), (1, 2), (3, 2), (5, 2), (7, 1))
-Z_STEP = ()
+Z_STEP = (2, 3)
 A_STEP = (2, 3)
-X_FAR = (0, 1)
+X_FAR = (0, 1, 2, 3, 4)
+Z_FAR, A_FAR = (0, 0)
+VIA = ()
 STEPS = (
-    (('copy',), (), (('bz', 1, 1), ('bz', -1, 1), ('bx', 1, 0), ('bx', -1, 0), ('bx2', 2, 0), ('ax', 1), ('ax', -1), ('ax', 2), ('bz', 1, 2), ('bz', -1, 2), ('az', 1, 0, 1), ('az', -1, 0, 1), ('bz', 1, 3), ('bz', -1, 3))),
+    (('copy',), (), (('bz', 1, 1), ('bz', -1, 1), ('bx', 1, 0), ('bx', -1, 0), ('bx2', 2, 0), ('ax', 1), ('ax', -1), ('ax', 2), ('az', 1, 0, 1), ('az', -1, 0, 1))),
     (('dq', 0), (), ()),
     (('dq', 1), (), ()),
     (('dq', 2), (), ()),
@@ -49,119 +52,120 @@
     (('dq', 5), (), ()),
     (('dq', 6), (), ()),
     (('dq', 7), (), ()),
+    (('copy',), (('bz', 1, 1),), (('bz', 1, 2),)),
+    (('copy',), (('bz', -1, 1),), (('bx', 1, 1), ('bx', -1, 1), ('bx2', 2, 1))),
+    (('copy',), (), (('bz', -1, 2),)),
     (('dq', 8), (), ()),
-    (('copy',), (('bz', 1, 1), ('bz', -1, 1)), (('bx', 1, 1), ('bx', -1, 1), ('bx2', 2, 1))),
+    (('copy',), (('az', 1, 0, 1),), (('az', 1, 0, 2),)),
+    (('copy',), (('az', -1, 0, 1),), (('az', -1, 0, 2),)),
     (('dq', 9), (), ()),
     (('copy',), (('ax', 1), ('ax', -1)), (('az', 1, 1, 1), ('az', -1, 1, 1))),
-    (('copy',), (('az', 1, 0, 1),), (('az', 1, 0, 2),)),
-    (('copy',), (('az', -1, 0, 1),), (('az', -1, 0, 2),)),
-    (('copy',), (('ax', 2), ('bx', 1, 0), ('bx', -1, 0), ('bx2', 2, 0)), (('sh', 0),)),
+    (('copy',), (('bx', 1, 0), ('bx', -1, 0), ('bx2', 2, 0)), (('shb', 0),)),
+    (('copy',), (('ax', 2),), (('sha', 0),)),
     (('copy',), (), (('az', 1, 2, 1), ('az', -1, 2, 1))),
     (('mma', 0, 0), (), ()),
     (('mma', 0, 1), (), ()),
     (('mma', 0, 2), (), ()),
-    (('copy',), (('bz', 1, 2), ('bz', -1, 2)), (('bx', 1, 2), ('bx', -1, 2))),
+    (('copy',), (('bz', 1, 2),), (('bz', 1, 3),)),
     (('mma', 0, 3), (), ()),
+    (('copy',), (('bz', -1, 2),), (('bx', 1, 2), ('bx', -1, 2), ('bx2', 2, 2))),
+    (('copy',), (), (('bz', -1, 3),)),
     (('mma', 0, 4), (), ()),
-    (('settle', 8), (), ()),
-    (('mmb', 0, 0), (('sh', 0),), ()),
+    (('copy',), (('az', 1, 0, 2),), (('az', 1, 0, 3),)),
+    (('copy',), (('az', -1, 0, 2),), (('az', -1, 0, 3),)),
+    (('settle', 5), (), ()),
+    (('mmb', 0, 0), (('sha', 0), ('shb', 0)), ()),
     (('mmb', 0, 1), (), ()),
-    (('copy',), (('bz', 1, 3),), (('bz4', 1),)),
-    (('copy',), (('bz', -1, 3),), (('bx', 1, 3), ('bx', -1, 3))),
-    (('copy',), (), (('bz4', -1),)),
     (('mmb', 0, 2), (), ()),
     (('mmb', 0, 3), (), ()),
     (('mmb', 0, 4), (), ()),
     (('scatter', 0), (), (('part', 2, 0), ('part', 1, 0), ('part', -1, 0))),
+    (('copy',), (('bx', 1, 1), ('bx', -1, 1), ('bx2', 2, 1)), (('shb', 1),)),
+    (('copy',), (('az', -1, 1, 1),), (('az', -1, 1, 2),)),
+    (('copy',), (('az', 1, 1, 1),), (('az', 1, 1, 2),)),
     (('tot', 0), (), ()),
-    (('settle', 6), (), ()),
-    (('copy',), (('az', 1, 1, 1),), (('az', 1, 1, 2),)),
-    (('copy',), (('az', -1, 1, 1),), (('az', -1, 1, 2),)),
-    (('copy',), (('az', 1, 0, 2),), (('az', 1, 0, 3),)),
-    (('copy',), (('az', -1, 0, 2),), (('az', -1, 0, 3),)),
-    (('settle', 3), (), ()),
+    (('settle', 5), (), ()),
     (('copy',), (('az', 1, 2, 1),), (('az', 1, 2, 2),)),
-    (('copy',), (('az', -1, 2, 1),), (('az', -1, 2, 2),)),
-    (('copy',), (('bx', -1, 2),), (('bx2', -1, 2),)),
-    (('copy',), (('bx', 1, 2),), (('bx2', 1, 2),)),
-    (('copy',), (('bx', 1, 1), ('bx', -1, 1), ('bx2', 2, 1)), (('sh', 1),)),
+    (('copy',), (('az', -1, 2, 1),), (('sha', 1),)),
+    (('copy',), (), (('az', -1, 2, 2),)),
     (('mma', 1, 0), (), ()),
     (('mma', 1, 1), (), ()),
-    (('copy',), (('bz4', 1), ('bz4', -1)), (('bx', 1, 4), ('bx', -1, 4))),
     (('mma', 1, 2), (), ()),
+    (('copy',), (('bz', 1, 3),), (('bz4', 1),)),
     (('mma', 1, 3), (), ()),
+    (('copy',), (('bz', -1, 3),), (('bz4', -1),)),
+    (('copy',), (), (('bx', 1, 3), ('bx', -1, 3), ('bx2', 2, 3))),
     (('mma', 1, 4), (), ()),
-    (('copy',), (('bx', 1, 3),), (('bx2', 1, 3),)),
-    (('copy',), (('bx', -1, 3),), (('bx2', -1, 3),)),
-    (('settle', 9), (), ()),
-    (('collect', 0), (('part', 1, 0), ('part', -1, 0), ('part', 2, 0)), ()),
+    (('copy',), (('az', 1, 0, 3),), (('az4', 1, 0),)),
+    (('copy',), (('az', -1, 0, 3),), (('az4', -1, 0),)),
+    (('settle', 10), (), ()),
+    (('copy',), (('bx', 1, 2), ('bx', -1, 2), ('bx2', 2, 2)), (('shb', 2),)),
+    (('mmb', 1, 0), (('sha', 1), ('shb', 1)), ()),
+    (('mmb', 1, 1), (), ()),
+    (('mmb', 1, 2), (), ()),
     (('copy',), (('az', 1, 1, 2),), (('az', 1, 1, 3),)),
     (('copy',), (('az', -1, 1, 2),), (('az', -1, 1, 3),)),
-    (('mmb', 1, 0), (('sh', 1),), ()),
-    (('mmb', 1, 1), (), ()),
-    (('mmb', 1, 2), (), ()),
     (('mmb', 1, 3), (), ()),
     (('mmb', 1, 4), (), ()),
     (('scatter', 1), (), (('part', 2, 1), ('part', 1, 1), ('part', -1, 1))),
-    (('copy',), (('az', 1, 0, 3),), (('az4', 1, 0),)),
-    (('copy',), (('az', -1, 0, 3),), (('az4', -1, 0),)),
     (('copy',), (('az', 1, 2, 2),), (('az', 1, 2, 3),)),
-    (('copy',), (('bx2', 1, 2), ('bx2', -1, 2), ('az', -1, 2, 2)), (('sh', 2),)),
-    (('copy',), (), (('az', -1, 2, 3),)),
-    (('copy',), (('bx', -1, 4),), (('bx2', -1, 4),)),
-    (('copy',), (('bx', 1, 4),), (('bx2', 1, 4),)),
-    (('tot', 1), (), ()),
+    (('copy',), (('az', -1, 2, 2),), (('az', -1, 2, 3),)),
+    (('copy',), (), (('sha', 2),)),
     (('mma', 2, 0), (), ()),
     (('mma', 2, 1), (), ()),
+    (('copy',), (('bz4', 1), ('bz4', -1)), (('bx', 1, 4), ('bx', -1, 4), ('bx2', 2, 4))),
+    (('tot', 1), (), ()),
     (('mma', 2, 2), (), ()),
     (('mma', 2, 3), (), ()),
     (('mma', 2, 4), (), ()),
-    (('settle', 11), (), ()),
-    (('mmb', 2, 0), (('sh', 2),), ()),
+    (('collect', 0), (('part', 1, 0), ('part', -1, 0), ('part', 2, 0)), ()),
+    (('settle', 16), (), ()),
+    (('copy',), (('bx', 1, 3), ('bx', -1, 3), ('bx2', 2, 3)), (('shb', 3),)),
+    (('mmb', 2, 0), (('sha', 2), ('shb', 2)), ()),
+    (('mmb', 2, 1), (), ()),
     (('copy',), (('az', 1, 1, 3),), (('az4', 1, 1),)),
-    (('mmb', 2, 1), (), ()),
     (('mmb', 2, 2), (), ()),
+    (('copy',), (('az', -1, 1, 3),), (('az4', -1, 1),)),
     (('mmb', 2, 3), (), ()),
     (('mmb', 2, 4), (), ()),
     (('scatter', 2), (), (('part', 2, 2), ('part', 1, 2), ('part', -1, 2))),
-    (('copy',), (('az', 1, 2, 3),), (('az4', 1, 2),)),
-    (('copy',), (('bx2', 1, 3), ('bx2', -1, 3), ('az', -1, 1, 3), ('az', -1, 2, 3)), (('sh', 3),)),
-    (('copy',), (), (('az4', -1, 2),)),
+    (('copy',), (('az', -1, 2, 3),), (('az4', -1, 2),)),
+    (('copy',), (('az', 1, 2, 3),), (('sha', 3),)),
     (('mma', 3, 0), (), ()),
+    (('copy',), (), (('az4', 1, 2),)),
     (('mma', 3, 1), (), ()),
     (('mma', 3, 2), (), ()),
+    (('copy',), (('bx', 1, 4), ('bx', -1, 4), ('bx2', 2, 4)), (('shb', 4),)),
+    (('tot', 2), (), ()),
     (('mma', 3, 3), (), ()),
-    (('copy',), (), (('az4', -1, 1),)),
-    (('tot', 2), (), ()),
     (('mma', 3, 4), (), ()),
-    (('settle', 11), (), ()),
+    (('settle', 8), (), ()),
     (('collect', 1), (('part', 1, 1), ('part', -1, 1), ('part', 2, 1)), ()),
-    (('mmb', 3, 0), (('sh', 3),), ()),
+    (('settle', 5), (), ()),
+    (('mmb', 3, 0), (('sha', 3), ('shb', 3)), ()),
     (('mmb', 3, 1), (), ()),
+    (('copy',), (('az4', 1, 0), ('az4', -1, 0), ('az4', 1, 1), ('az4', -1, 1), ('az4', 1, 2), ('az4', -1, 2)), (('sha', 4),)),
     (('mmb', 3, 2), (), ()),
     (('mmb', 3, 3), (), ()),
     (('mmb', 3, 4), (), ()),
     (('scatter', 3), (), (('part', 2, 3), ('part', 1, 3), ('part', -1, 3))),
-    (('tot', 3), (), ()),
-    (('settle', 6), (), ()),
-    (('copy',), (('bx2', 1, 4), ('bx2', -1, 4), ('az4', 1, 0), ('az4', 1, 1), ('az4', 1, 2), ('az4', -1, 0), ('az4', -1, 1), ('az4', -1, 2)), (('sh', 4),)),
     (('mma', 4, 0), (), ()),
     (('mma', 4, 1), (), ()),
     (('mma', 4, 2), (), ()),
     (('mma', 4, 3), (), ()),
     (('mma', 4, 4), (), ()),
-    (('settle', 5), (), ()),
-    (('mmb', 4, 0), (('sh', 4),), ()),
-    (('collect', 2), (('part', 1, 2), ('part', -1, 2), ('part', 2, 2)), ()),
+    (('tot', 3), (), ()),
+    (('mmb', 4, 0), (('sha', 4), ('shb', 4)), ()),
     (('mmb', 4, 1), (), ()),
     (('mmb', 4, 2), (), ()),
     (('mmb', 4, 3), (), ()),
     (('mmb', 4, 4), (), ()),
     (('scatter', 4), (), (('part', 2, 4), ('part', 1, 4), ('part', -1, 4))),
+    (('collect', 2), (('part', 1, 2), ('part', -1, 2), ('part', 2, 2)), ()),
     (('tot', 4), (), (('tot', 1), ('tot', -1), ('tot', 2))),
-    (('settle', 7), (), ()),
+    (('settle', 20), (), ()),
     (('collect', 3), (('part', 1, 3), ('part', -1, 3), ('part', 2, 3)), ()),
-    (('settle', 4), (), ()),
+    (('settle', 3), (), ()),
     (('collect', 4), (('part', 1, 4), ('part', -1, 4), ('part', 2, 4)), ()),
 )
 
@@ -215,11 +219,11 @@
 
 def kernel(
     q_hbm, mant_hbm, exps_hbm, bo_hbm, bi_hbm, eig_hbm, asg_hbm,
-    scores_hbm, totals_ref,
+    scores_ref, totals_ref,
     q_ref, exps_ref, bo_ref, bi_ref, eig_ref, asg_ref,
     mant, w, p, acc, fac, mask, bd, mid, prep, xch,
-    part_out, part_in, sums, tot, tot_in, out,
-    ss, rs, ls, ms, os,
+    part_out, part_in, sums, tot, tot_in,
+    ss, rs, ls, ms,
 ):
     e, y = lax.axis_index("ex"), lax.axis_index("lay")
     x, z, c = e // 16, (e // 2) % NZ, e % 2
@@ -256,7 +260,10 @@
         cp.start()
     barrier = pltpu.get_barrier_semaphore()
     partners = [at_x(d) for d in (1, -1, 2)] + [at_y(d) for d in (1, -1, 2)]
-    partners += [at_z(d * k) for k in (1, 2, 3) for d in (1, -1)] + [sibling]
+    steps = {1} | {k for k in (2, 3) if k not in Z_STEP or k not in A_STEP}
+    partners += [at_z(d * k) for k in sorted(steps) for d in (1, -1)] + [sibling]
+    if Z_FAR or A_FAR:
+        partners.append(at_z(4))
     for dev in partners:
         pl.semaphore_signal(barrier, inc=1, device_id=dev, device_id_type=MESH)
 
@@ -294,7 +301,10 @@
             remote(
                 ("bz", d, k), p.at[hops[via], 0, :, lb], p.at[hops[k], 0, :, lb], at_z(d * (k - via))
             )
-        remote(("bz4", d), p.at[hops[3], 0, :, lb2], p.at[ZSLOT[4], 0, :, lb2], at_z(d))
+        if not Z_FAR:
+            remote(("bz4", d), p.at[hops[3], 0, :, lb2], p.at[ZSLOT[4], 0, :, lb2], at_z(d))
+        elif d == 1:
+            remote(("bz4", 2), p.at[0, 0, :, lb], p.at[ZSLOT[4], 0, :, lb], at_z(4))
         for i, (first, count) in enumerate(XBLK):
             blk = pl.ds(first, count)
             for k in (1, 2, 3):
@@ -303,7 +313,12 @@
                     ("az", d, i, k),
                     p.at[hops[via], blk, :, la], p.at[hops[k], blk, :, la], at_z(d * (k - via)),
                 )
-            remote(("az4", d, i), p.at[hops[3], blk, :, la2], p.at[ZSLOT[4], blk, :, la2], at_z(d))
+            if not A_FAR:
+                remote(
+                    ("az4", d, i), p.at[hops[3], blk, :, la2], p.at[ZSLOT[4], blk, :, la2], at_z(d)
+                )
+            elif d == 1:
+                remote(("az4", 2, i), p.at[0, blk, :, la], p.at[ZSLOT[4], blk, :, la], at_z(4))
         near = XSLOT[(-d) % NX]
         for i, (first, count) in enumerate(DIST):
             blk = pl.ds(first, count)
@@ -316,9 +331,18 @@
     remote(("ax", 2), p.at[0, 0, :, la], p.at[0, 3, :, la], at_x(2))
     for g, (first, count) in enumerate(GROUP):
         blk = pl.ds(first, count)
-        remote(("sh", g), p.at[blk, :, :, lhalf], p.at[blk, :, :, lhalf], sibling)
-        for i, d in enumerate((1, -1, 2)):
-            remote(("part", d, g), part_out.at[i, blk], part_in.at[i, blk], at_y(d))
+        remote(("sha", g), p.at[blk, :, :, la], p.at[blk, :, :, la], sibling)
+        remote(("shb", g), p.at[blk, :, :, lb], p.at[blk, :, :, lb], sibling)
+        if g in VIA:
+            for i, d in enumerate((1, -1)):
+                t = pl.ds(i * HT, HT)
+                remote(
+                    ("y2", d, g), part_out.at[2, blk, :, t], part_in.at[2, blk, :, t], at_y(d)
+                )
+                remote(("y1", d, g), part_out.at[i, blk], part_in.at[i, blk], at_y(d))
+        else:
+            for i, d in enumerate((1, -1, 2)):
+                remote(("part", d, g), part_out.at[i, blk], part_in.at[i, blk], at_y(d))
     for i, d in enumerate((1, -1, 2)):
         remote(("tot", d), tot, tot_in.at[i], at_y(d))
     other_cols = pl.ds(pl.multiple_of((1 - c) * HALF, HALF), HALF)
@@ -388,35 +412,40 @@
 
     def scatter(g):
         first, count = GROUP[g]
-        for i, d in ((2, 2), (0, 1), (1, -1)):
+        for i, d in ((2, 2),) if g in VIA else ((2, 2), (0, 1), (1, -1)):
             to = slot_of(d)
             for s in range(first, first + count):
                 part_out[i, s] = acc[s, to].astype(bf16)
 
+    def combine(g):
+        first, count = GROUP[g]
+        for i, d in ((0, 1), (1, -1)):
+            to = slot_of(d)
+            for j in range(2):
+                t = pl.ds(j * HT, HT)
+                for s in range(first, first + count):
+                    v = acc[s, to, :, t]
+                    v = v + part_in[2, s, :, t].astype(f32) if i == j else v
+                    part_out[i, s, :, t] = v.astype(bf16)
+
     normalizer = 1.0 / math.sqrt(NY * ENTRIES)
-    stores = []
 
     def collect(g):
         mine = slot_of(0)
         first, count = GROUP[g]
         for s in range(first, first + count):
             total = acc[s, mine] + part_in[0, s].astype(f32)
-            total = total + part_in[1, s].astype(f32) + part_in[2, s].astype(f32)
-            out[s] = total * normalizer
+            total = total + part_in[1, s].astype(f32)
+            if g not in VIA:
+                total = total + part_in[2, s].astype(f32)
             zo = (z + ZORDER[s]) % NZ
-            cp = pltpu.make_async_copy(
-                out.at[s],
-                scores_hbm.at[pl.ds(pl.multiple_of(zo * PAIR, PAIR), PAIR)],
-                os.at[s],
-            )
-            cp.start()
-            stores.append(cp)
+            scores_ref[pl.ds(pl.multiple_of(zo * PAIR, PAIR), PAIR), :] = total * normalizer
 
     do = {
         "copy": lambda: None, "settle": lambda n: settle(max(len(live) - n, 0)),
         "dq": lambda i: None if i < EARLY else dequantize(i),
         "mma": lambda g, n: multiply(g, n, 0), "mmb": lambda g, n: multiply(g, n, 1),
-        "scatter": scatter, "tot": add_totals, "collect": collect,
+        "scatter": scatter, "comb": combine, "tot": add_totals, "collect": collect,
     }
     xch[c] = prep[:, own_cols]
     for i in range(EARLY):
@@ -437,11 +466,9 @@
             row = total[8 * i + n : 8 * i + n + 1, :]
             totals_ref[i : i + 1, n * NT : (n + 1) * NT] = row * (normalizer / math.sqrt(QB))
     settle()
-    for cp in stores:
-        cp.wait()
-
-
-N_COPIES = 2 * (3 + 1 + 4 * len(XBLK) + 10 + 1) - len(X_FAR) + 1 + 4 * len(GROUP) + 3 + 1
+
+
+N_COPIES = 2 * (3 + 1 + 4 * len(XBLK) + 10 + 1) - len(X_FAR) - Z_FAR - A_FAR * len(XBLK) + 1 + 5 * len(GROUP) + len(VIA) + 3 + 1
 
 
 def body(queries, train_mantissa, scale_exponents, basis_out, basis_in, eigen, assignment):
@@ -452,11 +479,11 @@
     scores, totals = pl.pallas_call(
         kernel,
         out_shape=(
-            jax.ShapeDtypeStruct((NX * 32, ROWS), f32),
-            jax.ShapeDtypeStruct((2, ROWS), f32),
+            pltpu.VMEM((NX * 32, ROWS), f32),
+            pltpu.VMEM((2, ROWS), f32),
         ),
         in_specs=[hbm] * 7,
-        out_specs=(hbm, pl.BlockSpec(memory_space=pltpu.VMEM)),
+        out_specs=(pl.BlockSpec(memory_space=pltpu.VMEM),) * 2,
         scratch_shapes=[
             vmem((QDEV, ENTRIES), bf16),
             vmem((BLOCKS, ROWS), jnp.int32),
@@ -479,12 +506,10 @@
             vmem((2, 8, ROWS), f32),
             vmem((16, NT), f32),
             vmem((3, 16, NT), f32),
-            vmem((NZ, PAIR, ROWS), f32),
             dma((N_COPIES,)),
             dma((N_COPIES,)),
             dma((6,)),
             dma((NCH,)),
-            dma((NZ,)),
         ],
         compiler_params=pltpu.CompilerParams(
             collective_id=0, has_side_effects=True, vmem_limit_bytes=56 * 2**20

time: 49.3 us -> 46.5 us (0.943)
  local copies, waits for them, and re-layouts: 3.27 us -> 1.44 us
  Pallas kernels: 45.2 us -> 44.3 us
    unnamed x2, local copies, waits for them, and re-layouts: 3.27 us -> 1.44 us
    pallas_call x1, Pallas kernels: 45.2 us -> 44.3 us  [body(): pl.pallas_call(kernel, out_shape=(pltpu.VMEM((NX * 32, ROWS), f32), pltpu...]
where the time goes in v2:
time: 46.5 us; the launch traced here: 46.4 us
  Pallas kernels  44.3 us (95%)
  local copies, waits for them, and re-layouts  1.44 us (3%)
  between operations  0.64 us (1%)
    pallas_call x1, Pallas kernels, body(): pl.pallas_call(kernel, out_shape=(pltpu.VMEM((NX * 32, ROWS), f32), pltpu...  44.3 us
    unnamed x2, local copies, waits for them, and re-layouts  1.44 us

profile of v2, /device:TPU:1, one launch (start us, length us, event | category | flops | bytes accessed | tf_op | source)
XLA Modules:
  0.0 46.4 jit_solution(5728764593770202435)
XLA Ops:
  0.6 44.3 %influence.1 = (f32[128,1280]{1,0:T(8,128)S(1)}, f32[2,1280]{1,0:T(2,128)S(1)}) custom-call(bf16[8,4096]{1,0:T(8,128)(2,1)} %bitcast.11, bf16[1280,4096]{1,0:T(8,128)(2,1)} %bitcast.9, s32[32,1280]{1,0:T(8,128)} %bitcast.10, f32[64,64]{1,0:T(8,128)} %bitcast.12, f32[64,64]{1,0:T(8,128)} %bitcast.13, f32[64,64]{1,0:T(8,128)} %bitcast.14, s32[1,512]{1,0:T(1,128)} %bitcast.15), custom_call_target="tpu_custom_call" | custom-call | tf_op jit(solution)/shard_map/influence/pallas_call | solution.py:479
  44.9 0.8 %copy.11 = f32[128,1280]{1,0:T(8,128)} copy(f32[128,1280]{1,0:T(8,128)S(1)} %get-tuple-element.2) | data formatting | bytes 1310720
  45.8 0.6 %copy.12 = f32[2,1280]{1,0:T(2,128)} copy(f32[2,1280]{1,0:T(2,128)S(1)} %get-tuple-element.3) | data formatting | bytes 20480

commit v3 on v2

--- a/solution.py
+++ b/solution.py
@@ -26,6 +26,10 @@
 TCH = 128
 NCH = ROWS // TCH
 EARLY = 2
+(
+    COPY, SETTLE, DQ, MMA, MMB, SCATTER, COMB, TOT, COLLECT,
+    BZ, BZ4, BX, BX2, AX, AZ, AZ4, SHA, SHB, PART, Y1, Y2, SWAP,
+) = range(22)
 QB = 256
 lowest_exponent = -2
 highest_exponent = 2
@@ -43,130 +47,131 @@
 Z_FAR, A_FAR = (0, 0)
 VIA = ()
 STEPS = (
-    (('copy',), (), (('bz', 1, 1), ('bz', -1, 1), ('bx', 1, 0), ('bx', -1, 0), ('bx2', 2, 0), ('ax', 1), ('ax', -1), ('ax', 2), ('az', 1, 0, 1), ('az', -1, 0, 1))),
-    (('dq', 0), (), ()),
-    (('dq', 1), (), ()),
-    (('dq', 2), (), ()),
-    (('dq', 3), (), ()),
-    (('dq', 4), (), ()),
-    (('dq', 5), (), ()),
-    (('dq', 6), (), ()),
-    (('dq', 7), (), ()),
-    (('copy',), (('bz', 1, 1),), (('bz', 1, 2),)),
-    (('copy',), (('bz', -1, 1),), (('bx', 1, 1), ('bx', -1, 1), ('bx2', 2, 1))),
-    (('copy',), (), (('bz', -1, 2),)),
-    (('dq', 8), (), ()),
-    (('copy',), (('az', 1, 0, 1),), (('az', 1, 0, 2),)),
-    (('copy',), (('az', -1, 0, 1),), (('az', -1, 0, 2),)),
-    (('dq', 9), (), ()),
-    (('copy',), (('ax', 1), ('ax', -1)), (('az', 1, 1, 1), ('az', -1, 1, 1))),
-    (('copy',), (('bx', 1, 0), ('bx', -1, 0), ('bx2', 2, 0)), (('shb', 0),)),
-    (('copy',), (('ax', 2),), (('sha', 0),)),
-    (('copy',), (), (('az', 1, 2, 1), ('az', -1, 2, 1))),
-    (('mma', 0, 0), (), ()),
-    (('mma', 0, 1), (), ()),
-    (('mma', 0, 2), (), ()),
-    (('copy',), (('bz', 1, 2),), (('bz', 1, 3),)),
-    (('mma', 0, 3), (), ()),
-    (('copy',), (('bz', -1, 2),), (('bx', 1, 2), ('bx', -1, 2), ('bx2', 2, 2))),
-    (('copy',), (), (('bz', -1, 3),)),
-    (('mma', 0, 4), (), ()),
-    (('copy',), (('az', 1, 0, 2),), (('az', 1, 0, 3),)),
-    (('copy',), (('az', -1, 0, 2),), (('az', -1, 0, 3),)),
-    (('settle', 5), (), ()),
-    (('mmb', 0, 0), (('sha', 0), ('shb', 0)), ()),
-    (('mmb', 0, 1), (), ()),
-    (('mmb', 0, 2), (), ()),
-    (('mmb', 0, 3), (), ()),
-    (('mmb', 0, 4), (), ()),
-    (('scatter', 0), (), (('part', 2, 0), ('part', 1, 0), ('part', -1, 0))),
-    (('copy',), (('bx', 1, 1), ('bx', -1, 1), ('bx2', 2, 1)), (('shb', 1),)),
-    (('copy',), (('az', -1, 1, 1),), (('az', -1, 1, 2),)),
-    (('copy',), (('az', 1, 1, 1),), (('az', 1, 1, 2),)),
-    (('tot', 0), (), ()),
-    (('settle', 5), (), ()),
-    (('copy',), (('az', 1, 2, 1),), (('az', 1, 2, 2),)),
-    (('copy',), (('az', -1, 2, 1),), (('sha', 1),)),
-    (('copy',), (), (('az', -1, 2, 2),)),
-    (('mma', 1, 0), (), ()),
-    (('mma', 1, 1), (), ()),
-    (('mma', 1, 2), (), ()),
-    (('copy',), (('bz', 1, 3),), (('bz4', 1),)),
-    (('mma', 1, 3), (), ()),
-    (('copy',), (('bz', -1, 3),), (('bz4', -1),)),
-    (('copy',), (), (('bx', 1, 3), ('bx', -1, 3), ('bx2', 2, 3))),
-    (('mma', 1, 4), (), ()),
-    (('copy',), (('az', 1, 0, 3),), (('az4', 1, 0),)),
-    (('copy',), (('az', -1, 0, 3),), (('az4', -1, 0),)),
-    (('settle', 10), (), ()),
-    (('copy',), (('bx', 1, 2), ('bx', -1, 2), ('bx2', 2, 2)), (('shb', 2),)),
-    (('mmb', 1, 0), (('sha', 1), ('shb', 1)), ()),
-    (('mmb', 1, 1), (), ()),
-    (('mmb', 1, 2), (), ()),
-    (('copy',), (('az', 1, 1, 2),), (('az', 1, 1, 3),)),
-    (('copy',), (('az', -1, 1, 2),), (('az', -1, 1, 3),)),
-    (('mmb', 1, 3), (), ()),
-    (('mmb', 1, 4), (), ()),
-    (('scatter', 1), (), (('part', 2, 1), ('part', 1, 1), ('part', -1, 1))),
-    (('copy',), (('az', 1, 2, 2),), (('az', 1, 2, 3),)),
-    (('copy',), (('az', -1, 2, 2),), (('az', -1, 2, 3),)),
-    (('copy',), (), (('sha', 2),)),
-    (('mma', 2, 0), (), ()),
-    (('mma', 2, 1), (), ()),
-    (('copy',), (('bz4', 1), ('bz4', -1)), (('bx', 1, 4), ('bx', -1, 4), ('bx2', 2, 4))),
-    (('tot', 1), (), ()),
-    (('mma', 2, 2), (), ()),
-    (('mma', 2, 3), (), ()),
-    (('mma', 2, 4), (), ()),
-    (('collect', 0), (('part', 1, 0), ('part', -1, 0), ('part', 2, 0)), ()),
-    (('settle', 16), (), ()),
-    (('copy',), (('bx', 1, 3), ('bx', -1, 3), ('bx2', 2, 3)), (('shb', 3),)),
-    (('mmb', 2, 0), (('sha', 2), ('shb', 2)), ()),
-    (('mmb', 2, 1), (), ()),
-    (('copy',), (('az', 1, 1, 3),), (('az4', 1, 1),)),
-    (('mmb', 2, 2), (), ()),
-    (('copy',), (('az', -1, 1, 3),), (('az4', -1, 1),)),
-    (('mmb', 2, 3), (), ()),
-    (('mmb', 2, 4), (), ()),
-    (('scatter', 2), (), (('part', 2, 2), ('part', 1, 2), ('part', -1, 2))),
-    (('copy',), (('az', -1, 2, 3),), (('az4', -1, 2),)),
-    (('copy',), (('az', 1, 2, 3),), (('sha', 3),)),
-    (('mma', 3, 0), (), ()),
-    (('copy',), (), (('az4', 1, 2),)),
-    (('mma', 3, 1), (), ()),
-    (('mma', 3, 2), (), ()),
-    (('copy',), (('bx', 1, 4), ('bx', -1, 4), ('bx2', 2, 4)), (('shb', 4),)),
-    (('tot', 2), (), ()),
-    (('mma', 3, 3), (), ()),
-    (('mma', 3, 4), (), ()),
-    (('settle', 8), (), ()),
-    (('collect', 1), (('part', 1, 1), ('part', -1, 1), ('part', 2, 1)), ()),
-    (('settle', 5), (), ()),
-    (('mmb', 3, 0), (('sha', 3), ('shb', 3)), ()),
-    (('mmb', 3, 1), (), ()),
-    (('copy',), (('az4', 1, 0), ('az4', -1, 0), ('az4', 1, 1), ('az4', -1, 1), ('az4', 1, 2), ('az4', -1, 2)), (('sha', 4),)),
-    (('mmb', 3, 2), (), ()),
-    (('mmb', 3, 3), (), ()),
-    (('mmb', 3, 4), (), ()),
-    (('scatter', 3), (), (('part', 2, 3), ('part', 1, 3), ('part', -1, 3))),
-    (('mma', 4, 0), (), ()),
-    (('mma', 4, 1), (), ()),
-    (('mma', 4, 2), (), ()),
-    (('mma', 4, 3), (), ()),
-    (('mma', 4, 4), (), ()),
-    (('tot', 3), (), ()),
-    (('mmb', 4, 0), (('sha', 4), ('shb', 4)), ()),
-    (('mmb', 4, 1), (), ()),
-    (('mmb', 4, 2), (), ()),
-    (('mmb', 4, 3), (), ()),
-    (('mmb', 4, 4), (), ()),
-    (('scatter', 4), (), (('part', 2, 4), ('part', 1, 4), ('part', -1, 4))),
-    (('collect', 2), (('part', 1, 2), ('part', -1, 2), ('part', 2, 2)), ()),
-    (('tot', 4), (), (('tot', 1), ('tot', -1), ('tot', 2))),
-    (('settle', 20), (), ()),
-    (('collect', 3), (('part', 1, 3), ('part', -1, 3), ('part', 2, 3)), ()),
-    (('settle', 3), (), ()),
-    (('collect', 4), (('part', 1, 4), ('part', -1, 4), ('part', 2, 4)), ()),
+    ((COPY,), (), ((BZ, 1, 1), (BZ, -1, 1), (BX, 1, 0), (BX, -1, 0), (BX2, 2, 0), (AX, 1), (AX, -1), (AX, 2), (AZ, 1, 0, 1), (AZ, -1, 0, 1))),
+    ((DQ, 0), (), ()),
+    ((DQ, 1), (), ()),
+    ((DQ, 2), (), ()),
+    ((DQ, 3), (), ()),
+    ((DQ, 4), (), ()),
+    ((DQ, 5), (), ()),
+    ((DQ, 6), (), ()),
+    ((DQ, 7), (), ()),
+    ((COPY,), ((BZ, -1, 1),), ((BZ, -1, 2),)),
+    ((COPY,), ((BZ, 1, 1),), ((BX, 1, 1), (BX, -1, 1), (BX2, 2, 1))),
+    ((COPY,), (), ((BZ, 1, 2),)),
+    ((DQ, 8), (), ()),
+    ((COPY,), ((AZ, 1, 0, 1),), ((AZ, 1, 0, 2),)),
+    ((DQ, 9), (), ()),
+    ((COPY,), ((AZ, -1, 0, 1),), ((AZ, -1, 0, 2),)),
+    ((COPY,), ((AX, 1), (AX, -1)), ((AZ, 1, 1, 1), (AZ, -1, 1, 1))),
+    ((COPY,), ((BX, 1, 0), (BX, -1, 0), (BX2, 2, 0)), ((SHB, 0),)),
+    ((COPY,), ((AX, 2),), ((SHA, 0),)),
+    ((COPY,), (), ((AZ, 1, 2, 1), (AZ, -1, 2, 1))),
+    ((MMA, 0, 0), (), ()),
+    ((MMA, 0, 1), (), ()),
+    ((MMA, 0, 2), (), ()),
+    ((COPY,), ((BZ, -1, 2),), ((BZ, -1, 3),)),
+    ((MMA, 0, 3), (), ()),
+    ((COPY,), ((BZ, 1, 2),), ((BX, 1, 2), (BX, -1, 2), (BX2, 2, 2))),
+    ((COPY,), (), ((BZ, 1, 3),)),
+    ((MMA, 0, 4), (), ()),
+    ((SETTLE, 5), (), ()),
+    ((COPY,), ((AZ, 1, 0, 2),), ((AZ, 1, 0, 3),)),
+    ((COPY,), ((AZ, -1, 0, 2),), ((AZ, -1, 0, 3),)),
+    ((SETTLE, 5), (), ()),
+    ((COPY,), ((BX, 1, 1), (BX, -1, 1), (BX2, 2, 1)), ((SHB, 1),)),
+    ((COPY,), ((AZ, 1, 1, 1),), ((AZ, 1, 1, 2),)),
+    ((COPY,), ((AZ, -1, 1, 1),), ((AZ, -1, 1, 2),)),
+    ((MMB, 0, 0), ((SHA, 0), (SHB, 0)), ()),
+    ((MMB, 0, 1), (), ()),
+    ((MMB, 0, 2), (), ()),
+    ((MMB, 0, 3), (), ()),
+    ((MMB, 0, 4), (), ()),
+    ((SCATTER, 0), (), ((PART, 2, 0), (PART, 1, 0), (PART, -1, 0))),
+    ((COPY,), ((AZ, 1, 2, 1), (AZ, -1, 2, 1)), ((SHA, 1),)),
+    ((COPY,), (), ((AZ, 1, 2, 2),)),
+    ((COPY,), (), ((AZ, -1, 2, 2),)),
+    ((TOT, 0), (), ()),
+    ((COPY,), ((BZ, 1, 3), (BZ, -1, 3)), ((BX, 1, 3), (BX, -1, 3), (BX2, 2, 3))),
+    ((COPY,), (), ((BZ4, 1),)),
+    ((COPY,), (), ((BZ4, -1),)),
+    ((MMA, 1, 0), (), ()),
+    ((MMA, 1, 1), (), ()),
+    ((MMA, 1, 2), (), ()),
+    ((COPY,), ((AZ, 1, 0, 3),), ((AZ4, 1, 0),)),
+    ((COPY,), ((AZ, -1, 0, 3),), ((AZ4, -1, 0),)),
+    ((MMA, 1, 3), (), ()),
+    ((MMA, 1, 4), (), ()),
+    ((COPY,), ((BX, 1, 2), (BX, -1, 2), (BX2, 2, 2)), ((SHB, 2),)),
+    ((SETTLE, 13), (), ()),
+    ((COPY,), ((AZ, 1, 1, 2),), ((AZ, 1, 1, 3),)),
+    ((COPY,), ((AZ, -1, 1, 2),), ((AZ, -1, 1, 3),)),
+    ((SETTLE, 5), (), ()),
+    ((COPY,), ((AZ, 1, 2, 2),), ((AZ, 1, 2, 3),)),
+    ((COPY,), ((AZ, -1, 2, 2),), ((AZ, -1, 2, 3),)),
+    ((COPY,), (), ((SHA, 2),)),
+    ((MMA, 2, 0), (), ()),
+    ((MMB, 1, 0), ((SHA, 1), (SHB, 1)), ()),
+    ((MMB, 1, 1), (), ()),
+    ((MMB, 1, 2), (), ()),
+    ((MMB, 1, 3), (), ()),
+    ((MMB, 1, 4), (), ()),
+    ((SCATTER, 1), (), ((PART, 2, 1), (PART, 1, 1), (PART, -1, 1))),
+    ((MMA, 2, 1), (), ()),
+    ((COPY,), ((BZ4, 1), (BZ4, -1)), ((BX, 1, 4), (BX, -1, 4), (BX2, 2, 4))),
+    ((MMA, 2, 2), (), ()),
+    ((MMA, 2, 3), (), ()),
+    ((COPY,), ((BX, 1, 3), (BX, -1, 3), (BX2, 2, 3)), ((SHB, 3),)),
+    ((TOT, 1), (), ()),
+    ((COLLECT, 0), ((PART, 1, 0), (PART, -1, 0), (PART, 2, 0)), ()),
+    ((MMA, 2, 4), (), ()),
+    ((COPY,), ((AZ, 1, 1, 3),), ((AZ4, 1, 1),)),
+    ((COPY,), ((AZ, -1, 1, 3),), ((AZ4, -1, 1),)),
+    ((SETTLE, 12), (), ()),
+    ((COPY,), ((AZ, 1, 2, 3),), ((AZ4, 1, 2),)),
+    ((COPY,), ((AZ, -1, 2, 3),), ((AZ4, -1, 2),)),
+    ((COPY,), (), ((SHA, 3),)),
+    ((MMB, 2, 0), ((SHA, 2), (SHB, 2)), ()),
+    ((MMB, 2, 1), (), ()),
+    ((MMB, 2, 2), (), ()),
+    ((MMB, 2, 3), (), ()),
+    ((MMB, 2, 4), (), ()),
+    ((SCATTER, 2), (), ((PART, 2, 2), (PART, 1, 2), (PART, -1, 2))),
+    ((MMA, 3, 0), (), ()),
+    ((MMA, 3, 1), (), ()),
+    ((TOT, 2), (), ()),
+    ((MMA, 3, 2), (), ()),
+    ((COPY,), ((BX, 1, 4), (BX, -1, 4), (BX2, 2, 4)), ((SHB, 4),)),
+    ((MMA, 3, 3), (), ()),
+    ((MMA, 3, 4), (), ()),
+    ((COPY,), ((AZ4, 1, 0), (AZ4, -1, 0), (AZ4, 1, 1), (AZ4, -1, 1), (AZ4, 1, 2), (AZ4, -1, 2)), ((SHA, 4),)),
+    ((MMA, 4, 0), (), ()),
+    ((MMA, 4, 1), (), ()),
+    ((MMA, 4, 2), (), ()),
+    ((MMA, 4, 3), (), ()),
+    ((MMA, 4, 4), (), ()),
+    ((COLLECT, 1), ((PART, 1, 1), (PART, -1, 1), (PART, 2, 1)), ()),
+    ((MMB, 3, 0), ((SHA, 3), (SHB, 3)), ()),
+    ((MMB, 3, 1), (), ()),
+    ((MMB, 3, 2), (), ()),
+    ((MMB, 3, 3), (), ()),
+    ((MMB, 3, 4), (), ()),
+    ((SCATTER, 3), (), ((PART, 2, 3), (PART, 1, 3), (PART, -1, 3))),
+    ((TOT, 3), (), ()),
+    ((SETTLE, 10), (), ()),
+    ((MMB, 4, 0), ((SHA, 4), (SHB, 4)), ()),
+    ((MMB, 4, 1), (), ()),
+    ((MMB, 4, 2), (), ()),
+    ((MMB, 4, 3), (), ()),
+    ((MMB, 4, 4), (), ()),
+    ((SCATTER, 4), (), ((PART, 2, 4), (PART, 1, 4), (PART, -1, 4))),
+    ((TOT, 4), (), ((TOT, 1), (TOT, -1), (TOT, 2))),
+    ((SETTLE, 8), (), ()),
+    ((COLLECT, 2), ((PART, 1, 2), (PART, -1, 2), (PART, 2, 2)), ()),
+    ((SETTLE, 14), (), ()),
+    ((COLLECT, 3), ((PART, 1, 3), (PART, -1, 3), (PART, 2, 3)), ()),
+    ((SETTLE, 6), (), ()),
+    ((COLLECT, 4), ((PART, 1, 4), (PART, -1, 4), (PART, 2, 4)), ()),
 )
 
 
@@ -299,61 +304,63 @@
         for k in (1, 2, 3):
             via = k - 1 if k in Z_STEP else 0
             remote(
-                ("bz", d, k), p.at[hops[via], 0, :, lb], p.at[hops[k], 0, :, lb], at_z(d * (k - via))
+                (BZ, d, k), p.at[hops[via], 0, :, lb], p.at[hops[k], 0, :, lb], at_z(d * (k - via))
             )
         if not Z_FAR:
-            remote(("bz4", d), p.at[hops[3], 0, :, lb2], p.at[ZSLOT[4], 0, :, lb2], at_z(d))
+            remote((BZ4, d), p.at[hops[3], 0, :, lb2], p.at[ZSLOT[4], 0, :, lb2], at_z(d))
         elif d == 1:
-            remote(("bz4", 2), p.at[0, 0, :, lb], p.at[ZSLOT[4], 0, :, lb], at_z(4))
+            remote((BZ4, 2), p.at[0, 0, :, lb], p.at[ZSLOT[4], 0, :, lb], at_z(4))
         for i, (first, count) in enumerate(XBLK):
             blk = pl.ds(first, count)
             for k in (1, 2, 3):
                 via = k - 1 if k in A_STEP else 0
                 remote(
-                    ("az", d, i, k),
+                    (AZ, d, i, k),
                     p.at[hops[via], blk, :, la], p.at[hops[k], blk, :, la], at_z(d * (k - via)),
                 )
             if not A_FAR:
                 remote(
-                    ("az4", d, i), p.at[hops[3], blk, :, la2], p.at[ZSLOT[4], blk, :, la2], at_z(d)
+                    (AZ4, d, i), p.at[hops[3], blk, :, la2], p.at[ZSLOT[4], blk, :, la2], at_z(d)
                 )
             elif d == 1:
-                remote(("az4", 2, i), p.at[0, blk, :, la], p.at[ZSLOT[4], blk, :, la], at_z(4))
+                remote((AZ4, 2, i), p.at[0, blk, :, la], p.at[ZSLOT[4], blk, :, la], at_z(4))
         near = XSLOT[(-d) % NX]
         for i, (first, count) in enumerate(DIST):
             blk = pl.ds(first, count)
-            remote(("bx", d, i), p.at[blk, 0, :, lb], p.at[blk, near, :, lb], at_x(d))
+            remote((BX, d, i), p.at[blk, 0, :, lb], p.at[blk, near, :, lb], at_x(d))
             if i not in X_FAR:
-                remote(("bx2", d, i), p.at[blk, near, :, lb2], p.at[blk, 3, :, lb2], at_x(d))
+                remote((BX2, d, i), p.at[blk, near, :, lb2], p.at[blk, 3, :, lb2], at_x(d))
             elif d == 1:
-                remote(("bx2", 2, i), p.at[blk, 0, :, lb], p.at[blk, 3, :, lb], at_x(2))
-        remote(("ax", d), p.at[0, 0, :, la], p.at[0, near, :, la], at_x(d))
-    remote(("ax", 2), p.at[0, 0, :, la], p.at[0, 3, :, la], at_x(2))
+                remote((BX2, 2, i), p.at[blk, 0, :, lb], p.at[blk, 3, :, lb], at_x(2))
+        remote((AX, d), p.at[0, 0, :, la], p.at[0, near, :, la], at_x(d))
+    remote((AX, 2), p.at[0, 0, :, la], p.at[0, 3, :, la], at_x(2))
     for g, (first, count) in enumerate(GROUP):
         blk = pl.ds(first, count)
-        remote(("sha", g), p.at[blk, :, :, la], p.at[blk, :, :, la], sibling)
-        remote(("shb", g), p.at[blk, :, :, lb], p.at[blk, :, :, lb], sibling)
+        remote((SHA, g), p.at[blk, :, :, la], p.at[blk, :, :, la], sibling)
+        remote((SHB, g), p.at[blk, :, :, lb], p.at[blk, :, :, lb], sibling)
         if g in VIA:
             for i, d in enumerate((1, -1)):
                 t = pl.ds(i * HT, HT)
                 remote(
-                    ("y2", d, g), part_out.at[2, blk, :, t], part_in.at[2, blk, :, t], at_y(d)
+                    (Y2, d, g), part_out.at[2, blk, :, t], part_in.at[2, blk, :, t], at_y(d)
                 )
-                remote(("y1", d, g), part_out.at[i, blk], part_in.at[i, blk], at_y(d))
+                remote((Y1, d, g), part_out.at[i, blk], part_in.at[i, blk], at_y(d))
         else:
             for i, d in enumerate((1, -1, 2)):
-                remote(("part", d, g), part_out.at[i, blk], part_in.at[i, blk], at_y(d))
+                remote((PART, d, g), part_out.at[i, blk], part_in.at[i, blk], at_y(d))
     for i, d in enumerate((1, -1, 2)):
-        remote(("tot", d), tot, tot_in.at[i], at_y(d))
+        remote((TOT, d), tot, tot_in.at[i], at_y(d))
     other_cols = pl.ds(pl.multiple_of((1 - c) * HALF, HALF), HALF)
     own_cols = pl.ds(pl.multiple_of(c * HALF, HALF), HALF)
-    remote(("swap",), prep.at[:, other_cols], xch.at[c], sibling)
-
-    for cp in small:
+    remote((SWAP,), prep.at[:, other_cols], xch.at[c], sibling)
+
+    for cp in small[:4]:
         cp.wait()
     precondition(q_ref, bo_ref, bi_ref, eig_ref, bd, mid, prep)
     pl.semaphore_wait(barrier, len(partners))
-    send("swap")
+    send(SWAP)
+    for cp in small[4:]:
+        cp.wait()
     exps = exps_ref[...]
     factor = jnp.zeros(exps.shape, f32)
     for exponent in range(lowest_exponent, highest_exponent):
@@ -442,24 +449,26 @@
             scores_ref[pl.ds(pl.multiple_of(zo * PAIR, PAIR), PAIR), :] = total * normalizer
 
     do = {
-        "copy": lambda: None, "settle": lambda n: settle(max(len(live) - n, 0)),
-        "dq": lambda i: None if i < EARLY else dequantize(i),
-        "mma": lambda g, n: multiply(g, n, 0), "mmb": lambda g, n: multiply(g, n, 1),
-        "scatter": scatter, "comb": combine, "tot": add_totals, "collect": collect,
+        COPY: lambda: None, SETTLE: lambda n: settle(max(len(live) - n, 0)),
+        DQ: lambda i: None if i < EARLY else dequantize(i),
+        MMA: lambda g, n: multiply(g, n, 0), MMB: lambda g, n: multiply(g, n, 1),
+        SCATTER: scatter, COMB: combine, TOT: add_totals, COLLECT: collect,
     }
     xch[c] = prep[:, own_cols]
     for i in range(EARLY):
         dequantize(i)
-    arrived("swap")
+    arrived(SWAP)
     p[0, 0, :, lhalf] = xch[...].reshape(PAIR, HALF).astype(bf16)
-    for (step, *args), waits, sends in STEPS:
+    for i, ((step, *args), waits, sends) in enumerate(STEPS):
+        if i == len(STEPS) - 1:
+            settle(6)
         for name in waits:
             arrived(*name)
         do[step](*args)
         for name in sends:
             send(*name)
     for d in (1, -1, 2):
-        arrived("tot", d)
+        arrived(TOT, d)
     total = tot[...] + tot_in[0] + tot_in[1] + tot_in[2]
     for i in range(2):
         for n in range(ROWS // NT):

time: 46.5 us -> 45.5 us (0.978)
  Pallas kernels: 44.3 us -> 43.2 us
    pallas_call x1, Pallas kernels: 44.3 us -> 43.2 us  [body(): pl.pallas_call(kernel, out_shape=(pltpu.VMEM((NX * 32, ROWS), f32), pltpu...]
where the time goes in v3:
time: 45.5 us; the launch traced here: 45.2 us
  Pallas kernels  43.2 us (95%)
  local copies, waits for them, and re-layouts  1.44 us (3%)
  between operations  0.64 us (1%)
    pallas_call x1, Pallas kernels, body(): pl.pallas_call(kernel, out_shape=(pltpu.VMEM((NX * 32, ROWS), f32), pltpu...  43.2 us
    unnamed x2, local copies, waits for them, and re-layouts  1.44 us

profile of v3, /device:TPU:1, one launch (start us, length us, event | category | flops | bytes accessed | tf_op | source)
XLA Modules:
  0.0 45.2 jit_solution(1272171388985861246)
XLA Ops:
  0.6 43.2 %influence.1 = (f32[128,1280]{1,0:T(8,128)S(1)}, f32[2,1280]{1,0:T(2,128)S(1)}) custom-call(bf16[8,4096]{1,0:T(8,128)(2,1)} %bitcast.11, bf16[1280,4096]{1,0:T(8,128)(2,1)} %bitcast.9, s32[32,1280]{1,0:T(8,128)} %bitcast.10, f32[64,64]{1,0:T(8,128)} %bitcast.12, f32[64,64]{1,0:T(8,128)} %bitcast.13, f32[64,64]{1,0:T(8,128)} %bitcast.14, s32[1,512]{1,0:T(1,128)} %bitcast.15), custom_call_target="tpu_custom_call" | custom-call | tf_op jit(solution)/shard_map/influence/pallas_call | solution.py:488
  43.8 0.8 %copy.11 = f32[128,1280]{1,0:T(8,128)} copy(f32[128,1280]{1,0:T(8,128)S(1)} %get-tuple-element.2) | data formatting | bytes 1310720
  44.6 0.6 %copy.12 = f32[2,1280]{1,0:T(2,128)} copy(f32[2,1280]{1,0:T(2,128)S(1)} %get-tuple-element.3) | data formatting | bytes 20480

commit v4 on v3

--- a/solution.py
+++ b/solution.py
@@ -19,7 +19,7 @@
 ROWS = 1280
 QDEV = 8
 PAIR = 16
-KA = 1024
+KA = 768
 KB = HALF - KA
 NT = 256
 HT = ROWS // 2
@@ -41,13 +41,15 @@
 XBLK = ((0, 1), (1, 2), (3, 1))
 DIST = ((0, 1), (1, 2), (3, 2), (5, 2), (7, 1))
 GROUP = ((0, 1), (1, 2), (3, 2), (5, 2), (7, 1))
-Z_STEP = (2, 3)
+Z_STEP = (3,)
 A_STEP = (2, 3)
 X_FAR = (0, 1, 2, 3, 4)
 Z_FAR, A_FAR = (0, 0)
 VIA = ()
 STEPS = (
-    ((COPY,), (), ((BZ, 1, 1), (BZ, -1, 1), (BX, 1, 0), (BX, -1, 0), (BX2, 2, 0), (AX, 1), (AX, -1), (AX, 2), (AZ, 1, 0, 1), (AZ, -1, 0, 1))),
+    ((COPY,), (), ((BZ, 1, 1), (BZ, -1, 1), (BX, 1, 0), (BX, -1, 0), (BX2, 2, 0), (AX, 1), (AX, -1), (AX, 2), (BZ, 1, 2), (BZ, -1, 2), (AZ, 1, 0, 1), (AZ, -1, 0, 1))),
+    ((COPY,), (), ((SHB, 0, 0),)),
+    ((COPY,), (), ((SHA, 0, 0),)),
     ((DQ, 0), (), ()),
     ((DQ, 1), (), ()),
     ((DQ, 2), (), ()),
@@ -56,121 +58,134 @@
     ((DQ, 5), (), ()),
     ((DQ, 6), (), ()),
     ((DQ, 7), (), ()),
-    ((COPY,), ((BZ, -1, 1),), ((BZ, -1, 2),)),
-    ((COPY,), ((BZ, 1, 1),), ((BX, 1, 1), (BX, -1, 1), (BX2, 2, 1))),
-    ((COPY,), (), ((BZ, 1, 2),)),
+    ((COPY,), ((BZ, 1, 1), (BZ, -1, 1)), ((BX, 1, 1), (BX, -1, 1), (BX2, 2, 1))),
+    ((COPY,), ((BX, 1, 0), (BX, -1, 0)), ((SHB, 0, 1),)),
     ((DQ, 8), (), ()),
+    ((DQ, 9), (), ()),
+    ((COPY,), ((AX, 1), (AX, -1)), ((AZ, 1, 1, 1), (AZ, -1, 1, 1))),
+    ((COPY,), (), ((SHA, 0, 1),)),
+    ((COPY,), (), ((SHB, 1, 0),)),
     ((COPY,), ((AZ, 1, 0, 1),), ((AZ, 1, 0, 2),)),
-    ((DQ, 9), (), ()),
-    ((COPY,), ((AZ, -1, 0, 1),), ((AZ, -1, 0, 2),)),
-    ((COPY,), ((AX, 1), (AX, -1)), ((AZ, 1, 1, 1), (AZ, -1, 1, 1))),
-    ((COPY,), ((BX, 1, 0), (BX, -1, 0), (BX2, 2, 0)), ((SHB, 0),)),
-    ((COPY,), ((AX, 2),), ((SHA, 0),)),
+    ((COPY,), ((AZ, -1, 0, 1),), ((SHA, 1, 0),)),
+    ((COPY,), (), ((AZ, -1, 0, 2),)),
+    ((COPY,), ((BX2, 2, 0),), ((SHB, 0, 2),)),
+    ((COPY,), ((AX, 2),), ((SHA, 0, 2),)),
     ((COPY,), (), ((AZ, 1, 2, 1), (AZ, -1, 2, 1))),
     ((MMA, 0, 0), (), ()),
+    ((COPY,), ((BZ, -1, 2),), ((BZ, -1, 3),)),
+    ((COPY,), ((BZ, 1, 2),), ((SHB, 2, 0),)),
     ((MMA, 0, 1), (), ()),
+    ((COPY,), (), ((BZ, 1, 3),)),
+    ((COPY,), (), ((BX, 1, 2), (BX, -1, 2), (BX2, 2, 2))),
     ((MMA, 0, 2), (), ()),
-    ((COPY,), ((BZ, -1, 2),), ((BZ, -1, 3),)),
     ((MMA, 0, 3), (), ()),
-    ((COPY,), ((BZ, 1, 2),), ((BX, 1, 2), (BX, -1, 2), (BX2, 2, 2))),
-    ((COPY,), (), ((BZ, 1, 3),)),
     ((MMA, 0, 4), (), ()),
-    ((SETTLE, 5), (), ()),
-    ((COPY,), ((AZ, 1, 0, 2),), ((AZ, 1, 0, 3),)),
+    ((SETTLE, 14), (), ()),
+    ((COPY,), ((BX, 1, 1), (BX, -1, 1)), ((SHB, 1, 1),)),
+    ((COPY,), ((AZ, 1, 1, 1),), ((AZ, 1, 1, 2),)),
+    ((COPY,), ((AZ, -1, 1, 1),), ((SHA, 1, 1),)),
+    ((COPY,), (), ((AZ, -1, 1, 2),)),
+    ((MMB, 0, 0), ((SHA, 0, 0), (SHA, 0, 1), (SHA, 0, 2), (SHB, 0, 0), (SHB, 0, 1), (SHB, 0, 2)), ()),
     ((COPY,), ((AZ, -1, 0, 2),), ((AZ, -1, 0, 3),)),
-    ((SETTLE, 5), (), ()),
-    ((COPY,), ((BX, 1, 1), (BX, -1, 1), (BX2, 2, 1)), ((SHB, 1),)),
-    ((COPY,), ((AZ, 1, 1, 1),), ((AZ, 1, 1, 2),)),
-    ((COPY,), ((AZ, -1, 1, 1),), ((AZ, -1, 1, 2),)),
-    ((MMB, 0, 0), ((SHA, 0), (SHB, 0)), ()),
+    ((COPY,), ((AZ, 1, 0, 2),), ((SHA, 2, 0),)),
+    ((COPY,), (), ((AZ, 1, 0, 3),)),
     ((MMB, 0, 1), (), ()),
     ((MMB, 0, 2), (), ()),
+    ((COPY,), ((AZ, 1, 2, 1),), ((AZ, 1, 2, 2),)),
+    ((COPY,), ((AZ, -1, 2, 1),), ((SHA, 1, 2),)),
+    ((COPY,), (), ((AZ, -1, 2, 2),)),
     ((MMB, 0, 3), (), ()),
     ((MMB, 0, 4), (), ()),
+    ((COPY,), ((BX2, 2, 1),), ((SHB, 1, 2),)),
     ((SCATTER, 0), (), ((PART, 2, 0), (PART, 1, 0), (PART, -1, 0))),
-    ((COPY,), ((AZ, 1, 2, 1), (AZ, -1, 2, 1)), ((SHA, 1),)),
-    ((COPY,), (), ((AZ, 1, 2, 2),)),
-    ((COPY,), (), ((AZ, -1, 2, 2),)),
+    ((COPY,), ((BZ, 1, 3),), ((BZ4, 1),)),
+    ((COPY,), ((BZ, -1, 3),), ((BZ4, -1),)),
     ((TOT, 0), (), ()),
-    ((COPY,), ((BZ, 1, 3), (BZ, -1, 3)), ((BX, 1, 3), (BX, -1, 3), (BX2, 2, 3))),
-    ((COPY,), (), ((BZ4, 1),)),
-    ((COPY,), (), ((BZ4, -1),)),
+    ((COPY,), (), ((SHB, 3, 0),)),
+    ((COPY,), (), ((BX, 1, 3), (BX, -1, 3), (BX2, 2, 3))),
     ((MMA, 1, 0), (), ()),
     ((MMA, 1, 1), (), ()),
     ((MMA, 1, 2), (), ()),
-    ((COPY,), ((AZ, 1, 0, 3),), ((AZ4, 1, 0),)),
-    ((COPY,), ((AZ, -1, 0, 3),), ((AZ4, -1, 0),)),
     ((MMA, 1, 3), (), ()),
     ((MMA, 1, 4), (), ()),
-    ((COPY,), ((BX, 1, 2), (BX, -1, 2), (BX2, 2, 2)), ((SHB, 2),)),
-    ((SETTLE, 13), (), ()),
-    ((COPY,), ((AZ, 1, 1, 2),), ((AZ, 1, 1, 3),)),
     ((COPY,), ((AZ, -1, 1, 2),), ((AZ, -1, 1, 3),)),
-    ((SETTLE, 5), (), ()),
+    ((COPY,), ((AZ, 1, 1, 2),), ((SHA, 2, 1),)),
+    ((COPY,), (), ((AZ, 1, 1, 3),)),
+    ((COPY,), ((BX, 1, 2), (BX, -1, 2)), ((SHB, 2, 1),)),
+    ((COPY,), ((AZ, 1, 0, 3),), ((AZ4, 1, 0),)),
+    ((COPY,), ((AZ, -1, 0, 3),), ((SHA, 3, 0),)),
+    ((COPY,), (), ((AZ4, -1, 0),)),
+    ((SETTLE, 8), (), ()),
     ((COPY,), ((AZ, 1, 2, 2),), ((AZ, 1, 2, 3),)),
     ((COPY,), ((AZ, -1, 2, 2),), ((AZ, -1, 2, 3),)),
-    ((COPY,), (), ((SHA, 2),)),
-    ((MMA, 2, 0), (), ()),
-    ((MMB, 1, 0), ((SHA, 1), (SHB, 1)), ()),
+    ((COPY,), (), ((SHA, 2, 2),)),
+    ((MMB, 1, 0), ((SHA, 1, 0), (SHA, 1, 1), (SHA, 1, 2), (SHB, 1, 0), (SHB, 1, 1), (SHB, 1, 2)), ()),
     ((MMB, 1, 1), (), ()),
     ((MMB, 1, 2), (), ()),
     ((MMB, 1, 3), (), ()),
     ((MMB, 1, 4), (), ()),
+    ((COPY,), ((BX2, 2, 2),), ((SHB, 2, 2),)),
     ((SCATTER, 1), (), ((PART, 2, 1), (PART, 1, 1), (PART, -1, 1))),
+    ((COPY,), ((BZ4, 1), (BZ4, -1)), ((SHB, 4, 0),)),
+    ((COLLECT, 0), ((PART, 1, 0), (PART, -1, 0), (PART, 2, 0)), ()),
+    ((COPY,), (), ((BX, 1, 4), (BX, -1, 4), (BX2, 2, 4))),
+    ((MMA, 2, 0), (), ()),
     ((MMA, 2, 1), (), ()),
-    ((COPY,), ((BZ4, 1), (BZ4, -1)), ((BX, 1, 4), (BX, -1, 4), (BX2, 2, 4))),
     ((MMA, 2, 2), (), ()),
+    ((COPY,), ((AZ, 1, 1, 3), (AZ, -1, 1, 3)), ((SHA, 3, 1),)),
+    ((COPY,), (), ((AZ4, -1, 1),)),
+    ((COPY,), (), ((AZ4, 1, 1),)),
+    ((COPY,), ((AZ4, 1, 0), (AZ4, -1, 0)), ((SHA, 4, 0),)),
     ((MMA, 2, 3), (), ()),
-    ((COPY,), ((BX, 1, 3), (BX, -1, 3), (BX2, 2, 3)), ((SHB, 3),)),
+    ((MMA, 2, 4), (), ()),
     ((TOT, 1), (), ()),
-    ((COLLECT, 0), ((PART, 1, 0), (PART, -1, 0), (PART, 2, 0)), ()),
-    ((MMA, 2, 4), (), ()),
-    ((COPY,), ((AZ, 1, 1, 3),), ((AZ4, 1, 1),)),
-    ((COPY,), ((AZ, -1, 1, 3),), ((AZ4, -1, 1),)),
-    ((SETTLE, 12), (), ()),
-    ((COPY,), ((AZ, 1, 2, 3),), ((AZ4, 1, 2),)),
-    ((COPY,), ((AZ, -1, 2, 3),), ((AZ4, -1, 2),)),
-    ((COPY,), (), ((SHA, 3),)),
-    ((MMB, 2, 0), ((SHA, 2), (SHB, 2)), ()),
+    ((COPY,), ((AZ, 1, 2, 3), (AZ, -1, 2, 3)), ((SHA, 3, 2),)),
+    ((COPY,), (), ((AZ4, -1, 2),)),
+    ((COPY,), (), ((AZ4, 1, 2),)),
+    ((COPY,), ((BX, 1, 3), (BX, -1, 3)), ((SHB, 3, 1),)),
+    ((SETTLE, 9), (), ()),
+    ((MMB, 2, 0), ((SHA, 2, 0), (SHA, 2, 1), (SHA, 2, 2), (SHB, 2, 0), (SHB, 2, 1), (SHB, 2, 2)), ()),
     ((MMB, 2, 1), (), ()),
     ((MMB, 2, 2), (), ()),
     ((MMB, 2, 3), (), ()),
     ((MMB, 2, 4), (), ()),
     ((SCATTER, 2), (), ((PART, 2, 2), (PART, 1, 2), (PART, -1, 2))),
+    ((COPY,), ((BX2, 2, 3),), ((SHB, 3, 2),)),
     ((MMA, 3, 0), (), ()),
     ((MMA, 3, 1), (), ()),
-    ((TOT, 2), (), ()),
     ((MMA, 3, 2), (), ()),
-    ((COPY,), ((BX, 1, 4), (BX, -1, 4), (BX2, 2, 4)), ((SHB, 4),)),
+    ((COPY,), ((AZ4, 1, 2), (AZ4, -1, 2)), ((SHA, 4, 2),)),
     ((MMA, 3, 3), (), ()),
     ((MMA, 3, 4), (), ()),
-    ((COPY,), ((AZ4, 1, 0), (AZ4, -1, 0), (AZ4, 1, 1), (AZ4, -1, 1), (AZ4, 1, 2), (AZ4, -1, 2)), ((SHA, 4),)),
+    ((COPY,), ((BX, 1, 4), (BX, -1, 4)), ((SHB, 4, 1),)),
+    ((COPY,), ((AZ4, 1, 1), (AZ4, -1, 1)), ((SHA, 4, 1),)),
+    ((TOT, 2), (), ()),
+    ((SETTLE, 11), (), ()),
+    ((COPY,), ((BX2, 2, 4),), ((SHB, 4, 2),)),
     ((MMA, 4, 0), (), ()),
     ((MMA, 4, 1), (), ()),
     ((MMA, 4, 2), (), ()),
     ((MMA, 4, 3), (), ()),
     ((MMA, 4, 4), (), ()),
-    ((COLLECT, 1), ((PART, 1, 1), (PART, -1, 1), (PART, 2, 1)), ()),
-    ((MMB, 3, 0), ((SHA, 3), (SHB, 3)), ()),
+    ((MMB, 3, 0), ((SHA, 3, 0), (SHA, 3, 1), (SHA, 3, 2), (SHB, 3, 0), (SHB, 3, 1), (SHB, 3, 2)), ()),
     ((MMB, 3, 1), (), ()),
     ((MMB, 3, 2), (), ()),
     ((MMB, 3, 3), (), ()),
     ((MMB, 3, 4), (), ()),
     ((SCATTER, 3), (), ((PART, 2, 3), (PART, 1, 3), (PART, -1, 3))),
     ((TOT, 3), (), ()),
-    ((SETTLE, 10), (), ()),
-    ((MMB, 4, 0), ((SHA, 4), (SHB, 4)), ()),
+    ((COLLECT, 1), ((PART, 1, 1), (PART, -1, 1), (PART, 2, 1)), ()),
+    ((MMB, 4, 0), ((SHA, 4, 0), (SHA, 4, 1), (SHA, 4, 2), (SHB, 4, 0), (SHB, 4, 1), (SHB, 4, 2)), ()),
     ((MMB, 4, 1), (), ()),
     ((MMB, 4, 2), (), ()),
     ((MMB, 4, 3), (), ()),
     ((MMB, 4, 4), (), ()),
     ((SCATTER, 4), (), ((PART, 2, 4), (PART, 1, 4), (PART, -1, 4))),
     ((TOT, 4), (), ((TOT, 1), (TOT, -1), (TOT, 2))),
-    ((SETTLE, 8), (), ()),
     ((COLLECT, 2), ((PART, 1, 2), (PART, -1, 2), (PART, 2, 2)), ()),
-    ((SETTLE, 14), (), ()),
+    ((SETTLE, 47), (), ()),
     ((COLLECT, 3), ((PART, 1, 3), (PART, -1, 3), (PART, 2, 3)), ()),
-    ((SETTLE, 6), (), ()),
+    ((SETTLE, 9), (), ()),
     ((COLLECT, 4), ((PART, 1, 4), (PART, -1, 4), (PART, 2, 4)), ()),
 )
 
@@ -336,8 +351,10 @@
     remote((AX, 2), p.at[0, 0, :, la], p.at[0, 3, :, la], at_x(2))
     for g, (first, count) in enumerate(GROUP):
         blk = pl.ds(first, count)
-        remote((SHA, g), p.at[blk, :, :, la], p.at[blk, :, :, la], sibling)
-        remote((SHB, g), p.at[blk, :, :, lb], p.at[blk, :, :, lb], sibling)
+        for k, (low, wide) in enumerate(XBLK):
+            xs = pl.ds(low, wide)
+            remote((SHA, g, k), p.at[blk, xs, :, la], p.at[blk, xs, :, la], sibling)
+            remote((SHB, g, k), p.at[blk, xs, :, lb], p.at[blk, xs, :, lb], sibling)
         if g in VIA:
             for i, d in enumerate((1, -1)):
                 t = pl.ds(i * HT, HT)
@@ -477,7 +494,7 @@
     settle()
 
 
-N_COPIES = 2 * (3 + 1 + 4 * len(XBLK) + 10 + 1) - len(X_FAR) - Z_FAR - A_FAR * len(XBLK) + 1 + 5 * len(GROUP) + len(VIA) + 3 + 1
+N_COPIES = 2 * (3 + 1 + 4 * len(XBLK) + 10 + 1) - len(X_FAR) - Z_FAR - A_FAR * len(XBLK) + 1 + 9 * len(GROUP) + len(VIA) + 3 + 1
 
 
 def body(queries, train_mantissa, scale_exponents, basis_out, basis_in, eigen, assignment):

time: 45.5 us -> 45.7 us (level)
  no operation moved by 1% of the time
where the time goes in v4:
time: 45.7 us; the launch traced here: 45.4 us
  Pallas kernels  43.4 us (95%)
  local copies, waits for them, and re-layouts  1.44 us (3%)
  between operations  0.64 us (1%)
    pallas_call x1, Pallas kernels, body(): pl.pallas_call(kernel, out_shape=(pltpu.VMEM((NX * 32, ROWS), f32), pltpu...  43.4 us
    unnamed x2, local copies, waits for them, and re-layouts  1.44 us

profile of v4, /device:TPU:1, one launch (start us, length us, event | category | flops | bytes accessed | tf_op | source)
XLA Modules:
  0.0 45.4 jit_solution(15508634060505240619)
XLA Ops:
  0.6 43.4 %influence.1 = (f32[128,1280]{1,0:T(8,128)S(1)}, f32[2,1280]{1,0:T(2,128)S(1)}) custom-call(bf16[8,4096]{1,0:T(8,128)(2,1)} %bitcast.11, bf16[1280,4096]{1,0:T(8,128)(2,1)} %bitcast.9, s32[32,1280]{1,0:T(8,128)} %bitcast.10, f32[64,64]{1,0:T(8,128)} %bitcast.12, f32[64,64]{1,0:T(8,128)} %bitcast.13, f32[64,64]{1,0:T(8,128)} %bitcast.14, s32[1,512]{1,0:T(1,128)} %bitcast.15), custom_call_target="tpu_custom_call" | custom-call | tf_op jit(solution)/shard_map/influence/pallas_call | solution.py:505
  44.0 0.8 %copy.11 = f32[128,1280]{1,0:T(8,128)} copy(f32[128,1280]{1,0:T(8,128)S(1)} %get-tuple-element.2) | data formatting | bytes 1310720
  44.8 0.6 %copy.12 = f32[2,1280]{1,0:T(2,128)} copy(f32[2,1280]{1,0:T(2,128)S(1)} %get-tuple-element.3) | data formatting | bytes 20480

commit v5 on v3

--- a/solution.py
+++ b/solution.py
@@ -25,7 +25,7 @@
 HT = ROWS // 2
 TCH = 128
 NCH = ROWS // TCH
-EARLY = 2
+EARLY = 1
 (
     COPY, SETTLE, DQ, MMA, MMB, SCATTER, COMB, TOT, COLLECT,
     BZ, BZ4, BX, BX2, AX, AZ, AZ4, SHA, SHB, PART, Y1, Y2, SWAP,
@@ -261,8 +261,6 @@
         )
         for i in range(NCH)
     ]
-    for cp in loads:
-        cp.start()
     barrier = pltpu.get_barrier_semaphore()
     partners = [at_x(d) for d in (1, -1, 2)] + [at_y(d) for d in (1, -1, 2)]
     steps = {1} | {k for k in (2, 3) if k not in Z_STEP or k not in A_STEP}
@@ -271,6 +269,8 @@
         partners.append(at_z(4))
     for dev in partners:
         pl.semaphore_signal(barrier, inc=1, device_id=dev, device_id_type=MESH)
+    for cp in loads:
+        cp.start()
 
     copies, live = {}, []
 
@@ -366,9 +366,6 @@
     for exponent in range(lowest_exponent, highest_exponent):
         factor = factor + jnp.where(exps == exponent, f32(2.0**exponent), f32(0.0))
     fac[...] = factor
-    for i in range(NX):
-        one = (asg_ref[:, i * 128 : (i + 1) * 128] == 1).astype(f32)
-        mask[i] = jnp.broadcast_to(one, (128, 128)).T
 
     def dequantize(i):
         loads[i].wait()
@@ -460,6 +457,10 @@
     arrived(SWAP)
     p[0, 0, :, lhalf] = xch[...].reshape(PAIR, HALF).astype(bf16)
     for i, ((step, *args), waits, sends) in enumerate(STEPS):
+        if i == 1:
+            for j in range(NX):
+                one = (asg_ref[:, j * 128 : (j + 1) * 128] == 1).astype(f32)
+                mask[j] = jnp.broadcast_to(one, (128, 128)).T
         if i == len(STEPS) - 1:
             settle(6)
         for name in waits:

time: 45.5 us -> 42.9 us (0.943)
  Pallas kernels: 43.2 us -> 40.7 us
    pallas_call x1, Pallas kernels: 43.2 us -> 40.7 us  [body(): pl.pallas_call(kernel, out_shape=(pltpu.VMEM((NX * 32, ROWS), f32), pltpu...]
where the time goes in v5:
time: 42.9 us; the launch traced here: 42.8 us
  Pallas kernels  40.7 us (95%)
  local copies, waits for them, and re-layouts  1.44 us (3%)
  between operations  0.64 us (1%)
    pallas_call x1, Pallas kernels, body(): pl.pallas_call(kernel, out_shape=(pltpu.VMEM((NX * 32, ROWS), f32), pltpu...  40.7 us
    unnamed x2, local copies, waits for them, and re-layouts  1.44 us

profile of v5, /device:TPU:1, one launch (start us, length us, event | category | flops | bytes accessed | tf_op | source)
XLA Modules:
  0.0 42.8 jit_solution(10682003574889890888)
XLA Ops:
  0.6 40.7 %influence.1 = (f32[128,1280]{1,0:T(8,128)S(1)}, f32[2,1280]{1,0:T(2,128)S(1)}) custom-call(bf16[8,4096]{1,0:T(8,128)(2,1)} %bitcast.11, bf16[1280,4096]{1,0:T(8,128)(2,1)} %bitcast.9, s32[32,1280]{1,0:T(8,128)} %bitcast.10, f32[64,64]{1,0:T(8,128)} %bitcast.12, f32[64,64]{1,0:T(8,128)} %bitcast.13, f32[64,64]{1,0:T(8,128)} %bitcast.14, s32[1,512]{1,0:T(1,128)} %bitcast.15), custom_call_target="tpu_custom_call" | custom-call | tf_op jit(solution)/shard_map/influence/pallas_call | solution.py:489
  41.3 0.8 %copy.11 = f32[128,1280]{1,0:T(8,128)} copy(f32[128,1280]{1,0:T(8,128)S(1)} %get-tuple-element.2) | data formatting | bytes 1310720
  42.2 0.6 %copy.12 = f32[2,1280]{1,0:T(2,128)} copy(f32[2,1280]{1,0:T(2,128)S(1)} %get-tuple-element.3) | data formatting | bytes 20480
